TPU v7x, 128 devices: a whole 4x4x4 slice. The times are simulated.
128 devices in a mesh: tp: 2 (over core), ep: 64 (over y, x, z).
Axes of the slice: x: 4, y: 4, z: 4, core: 2. Of those that a mesh axis runs over, the one named last changes fastest.
Arguments:
- tokens: bfloat16 [16384, 4096], P(('tp', 'ep')), may hold values from -6 to 6
- upstream: bfloat16 [16384, 4096], P(('tp', 'ep')), may hold values from -4 to 4
- routes: int32 [16384, 2], P(('tp', 'ep')), may hold values from 0 to 63, all different within a row; in each aligned block of 128 rows (0 to 127, 128 to 255, ...) at most 8 rows name the same one
- route_weights: float32 [16384, 2], P(('tp', 'ep')), may hold values from 0.1 to 1
- gate_weight: bfloat16 [64, 4096, 768], P('ep', None, 'tp'), may hold values from -0.09375 to 0.09375
- up_weight: bfloat16 [64, 4096, 768], P('ep', None, 'tp'), may hold values from -0.09375 to 0.09375
- down_weight: bfloat16 [64, 768, 4096], P('ep', 'tp'), may hold values from -0.21875 to 0.21875
Outputs:
- mixed: bfloat16 [16384, 4096], P(('tp', 'ep'))
- grad_tokens: bfloat16 [16384, 4096], P(('tp', 'ep'))
- grad_route: float32 [16384, 2], P(('tp', 'ep'))
- grad_gate: bfloat16 [64, 4096, 768], P('ep', None, 'tp')
- grad_up: bfloat16 [64, 4096, 768], P('ep', None, 'tp')
- grad_down: bfloat16 [64, 768, 4096], P('ep', 'tp')
Inputs may be any that keep to these rules, and one draw needn't show every extreme that they name: `routes`: each row names 2 different experts. Among the 128 rows of one device no expert is named more than 8 times, a bound that some block reaches.
All inputs are finite; a program needn't handle non-finite values.
Results may differ from a plain program's by a relative error of at most 0.0072.
Values may be sent and summed in bfloat16 or wider, within the bound.
No kernel may reach another device: no remote copies, remote signals or barrier semaphores. Data moves between devices by JAX's collectives and lax.ppermute only.
A program may use at most 192 MiB of HBM per device.

v0:
```python
import jax
import jax.numpy as jnp
from jax import lax
from jax.sharding import PartitionSpec as P

TOP = 2
TOK_DEV = 128


def give_back(partials, capacity):
    stack_count = partials.shape[0]
    model_width = partials.shape[2]
    reshaped = partials.reshape(stack_count, -1, capacity, model_width)
    summed = lax.psum_scatter(reshaped.astype(jnp.bfloat16), "tp", scatter_dimension=1, tiled=True)
    return lax.all_to_all(summed, "ep", split_axis=1, concat_axis=1, tiled=True)


def on_device(tokens, upstream, routes, route_weights, gate_weight, up_weight, down_weight):
    ep_size = lax.axis_size("ep")
    capacity = 2 * TOK_DEV * TOP // ep_size
    row_count = tokens.shape[0]
    model_width = tokens.shape[1]
    top_count = routes.shape[1]
    expert_ids = jnp.arange(ep_size, dtype=jnp.int32)
    expert_hits = jnp.sum((routes[:, :, None] == expert_ids).astype(jnp.float32), axis=1)
    positions = jnp.arange(row_count, dtype=jnp.int32)
    earlier_mask = (positions[:, None] > positions[None, :]).astype(jnp.float32)
    prior_counts = jnp.dot(
        earlier_mask,
        expert_hits,
        precision=lax.Precision.HIGHEST,
        preferred_element_type=jnp.float32,
    )
    slot_index = jnp.take_along_axis(prior_counts, routes, axis=1).astype(jnp.int32)
    target_row = (routes * capacity + slot_index).reshape(-1)
    copied = jnp.repeat(tokens, top_count, axis=0)
    scaled_grads = (upstream.astype(jnp.float32)[:, None, :] * route_weights[:, :, None]).astype(
        jnp.bfloat16
    )
    scaled_grads = scaled_grads.reshape(row_count * top_count, model_width)
    outgoing = jnp.zeros((2, ep_size * capacity, model_width), jnp.bfloat16)
    outgoing = outgoing.at[:, target_row].set(jnp.stack([copied, scaled_grads]))
    outgoing = outgoing.reshape(2, ep_size, capacity, model_width)
    arrived = lax.all_to_all(outgoing, "ep", split_axis=1, concat_axis=1, tiled=True)
    arrived = lax.all_gather(arrived, "tp", axis=1, tiled=True)
    inputs = arrived[0].reshape(-1, model_width)
    grad_rows = arrived[1].reshape(-1, model_width)
    gate_mat = gate_weight[0]
    up_mat = up_weight[0]
    down_mat = down_weight[0]
    gate_pre = jnp.dot(inputs, gate_mat, preferred_element_type=jnp.float32)
    up_pre = jnp.dot(inputs, up_mat, preferred_element_type=jnp.float32)
    sigmoid_gate = jax.nn.sigmoid(gate_pre)
    active = gate_pre * sigmoid_gate
    hidden = (active * up_pre).astype(jnp.bfloat16)
    out_part = jnp.dot(hidden, down_mat, preferred_element_type=jnp.float32)
    forward_back = give_back(out_part[None], capacity)[0]
    d_hidden = jnp.dot(grad_rows, down_mat.T, preferred_element_type=jnp.float32)
    d_gate = (d_hidden * up_pre * sigmoid_gate * (1.0 + gate_pre * (1.0 - sigmoid_gate))).astype(
        jnp.bfloat16
    )
    d_up = (d_hidden * active).astype(jnp.bfloat16)
    grad_gate = jnp.dot(inputs.T, d_gate, preferred_element_type=jnp.float32).astype(jnp.bfloat16)
    grad_up = jnp.dot(inputs.T, d_up, preferred_element_type=jnp.float32).astype(jnp.bfloat16)
    grad_down = jnp.dot(hidden.T, grad_rows, preferred_element_type=jnp.float32).astype(
        jnp.bfloat16
    )
    back_part = jnp.dot(d_gate, gate_mat.T, preferred_element_type=jnp.float32) + jnp.dot(
        d_up, up_mat.T, preferred_element_type=jnp.float32
    )
    token_part = give_back(back_part[None], capacity)[0]
    expert_rows = forward_back.reshape(ep_size * capacity, model_width)[target_row]
    expert_rows = expert_rows.reshape(row_count, top_count, model_width).astype(jnp.float32)
    mixed = jnp.sum(route_weights[:, :, None] * expert_rows, axis=1).astype(jnp.bfloat16)
    grad_route = jnp.sum(upstream.astype(jnp.float32)[:, None, :] * expert_rows, axis=2)
    token_rows = token_part.reshape(ep_size * capacity, model_width)[target_row]
    token_rows = token_rows.reshape(row_count, top_count, model_width).astype(jnp.float32)
    grad_tokens = jnp.sum(token_rows, axis=1).astype(jnp.bfloat16)
    return (mixed, grad_tokens, grad_route, grad_gate[None], grad_up[None], grad_down[None])


def solution(mesh):
    return jax.shard_map(
        on_device,
        mesh=mesh,
        in_specs=(
            P(("tp", "ep"), None),
            P(("tp", "ep"), None),
            P(("tp", "ep"), None),
            P(("tp", "ep"), None),
            P("ep", None, "tp"),
            P("ep", None, "tp"),
            P("ep", "tp", None),
        ),
        out_specs=(
            P(("tp", "ep"), None),
            P(("tp", "ep"), None),
            P(("tp", "ep"), None),
            P("ep", None, "tp"),
            P("ep", None, "tp"),
            P("ep", "tp", None),
        ),
        check_vma=False,
    )
```

profile of v0, /device:TPU:2, one launch (start us, length us, event | category | flops | bytes accessed | tf_op | source)
XLA Modules:
  0.0 468.9 jit_solution(15563730371475620804)
XLA Ops:
  7.2 0.0 copy-start
  7.2 0.0 all-gather.2.cloned.1.call-start
  7.2 0.8 bitcast_or_fusion
  8.1 0.8 convert_reduce_fusion
  8.8 0.2 fusion.18
  9.0 0.1 copy.64
  9.1 0.1 reshape.148
  9.3 0.0 copy-start.9
  9.3 0.0 copy-start.10
  9.3 2.0 gather_fusion.2
  11.3 0.1 reshape.151
  11.4 0.1 copy.65
  11.5 0.1 copy.66
  11.6 0.1 reshape.128
  11.8 0.1 copy.63
  11.9 0.1 mul.74
  12.1 4.6 broadcast_in_dim.16
  16.7 4.1 stack_reshape.4
  20.8 5.3 %mul.72 = f32[128,2,4096]{2,1,0:T(2,128)} broadcast(bf16[128,4096]{1,0:T(8,128)(2,1)} %param.8), dimensions={0,2} | broadcast | bytes 5242880 | tf_op jit(solution)/shard_map/mul | solution.py:37
  26.1 6.1 %mul.73 = f32[1,256,4096]{2,1,0:T(8,128)} reshape(f32[128,2,4096]{2,1,0:T(2,128)} %mul.72) | data formatting | bytes 8388608 | tf_op jit(solution)/shard_map/mul | solution.py:37
  32.2 2.8 multiply_convert_fusion
  35.0 0.0 copy-done.2
  35.1 2.3 maximum_bitcast_fusion
  37.4 8.6 %copy.68 = bf16[256,2,4096]{2,1,0:T(2,128)(2,1)} copy(bf16[256,2,4096]{2,0,1:T(8,128)(2,1)} %maximum_bitcast_fusion) | data formatting | bytes 8388608 | tf_op jit(solution)/shard_map/stack | solution.py:42
  45.9 8.5 %broadcast_in_dim.14 = bf16[2,512,4096]{2,0,1:T(2,128)(2,1)} broadcast(bf16[]{:T(256)} %constant.9.clone.1), dimensions={} | broadcast | bytes 8388610 | tf_op jit(solution)/shard_map/broadcast_in_dim | solution.py:41
  54.5 34.6 %scatter_fusion = bf16[2,512,4096]{2,0,1:T(2,128)(2,1)} fusion(bf16[2,512,4096]{2,0,1:T(2,128)(2,1)} %broadcast_in_dim.14, s32[256]{0:T(256)S(1)} %bitcast.69, bf16[256,2,4096]{2,1,0:T(2,128)(2,1)} %copy.68), kind=kCustom, calls=%fused_computation.3 | custom fusion | bytes 12583936 | tf_op jit(solution)/shard_map/scatter | solution.py:42
  89.1 16.2 %copy.69 = bf16[2,64,8,4096]{3,2,0,1:T(8,128)(2,1)} copy(bf16[2,64,8,4096]{3,0,2,1:T(2,128)(2,1)} %bitcast.68) | data formatting | bytes 16777216 | tf_op jit(solution)/shard_map/reshape | solution.py:43
  105.4 107.8 %all_to_all.15 = bf16[2,64,8,4096]{3,2,0,1:T(8,128)(2,1)} all-to-all(bf16[2,64,8,4096]{3,2,0,1:T(8,128)(2,1)} %copy.69), channel_id=1, replica_groups=mesh['tp'=2,'ep'=64] {'ep'}, dimensions={1} | all-to-all | bytes 16777216 | tf_op jit(solution)/shard_map/all_to_all | solution.py:44
  213.2 7.7 %copy.70 = bf16[2,64,8,4096]{3,2,1,0:T(8,128)(2,1)} copy(bf16[2,64,8,4096]{3,2,0,1:T(8,128)(2,1)} %all_to_all.15) | data formatting | bytes 16777216 | tf_op jit(solution)/shard_map/all_to_all | solution.py:44
  220.9 0.0 all-gather.2.cloned.1.call-update
  220.9 0.0 reduce-scatter.3.cloned.1.call-start
  221.0 30.3 %all-gather.2.cloned.1.call-done = bf16[2,128,8,4096]{3,2,1,0:T(8,128)(2,1)} async-done(((bf16[2,64,8,4096]{3,2,1,0:T(8,128)(2,1)}), bf16[2,128,8,4096]{3,2,1,0:T(8,128)(2,1)}) %all-gather.2.cloned.1.call-update) | async-done | bytes 16777232 | tf_op jit(solution)/shard_map/all_gather | solution.py:45
  251.3 8.4 %fusion.4 = f32[1024,384]{1,0:T(8,128)S(1)} fusion(bf16[2,128,8,4096]{3,2,1,0:T(8,128)(2,1)} %all-gather.2.cloned.1.call-done, bf16[1,4096,384]{2,1,0:T(8,128)(2,1)} %param.12), kind=kOutput, calls=%fused_computation.14 | convolution fusion | flops 3221225472 | bytes 13107200 | tf_op jit(solution)/shard_map/dot_general | solution.py:52
  259.7 1.7 copy-done.11
  261.4 5.6 %fusion.5 = f32[1024,384]{1,0:T(8,128)} fusion(bf16[2,128,8,4096]{3,2,1,0:T(8,128)(2,1)S(1)} %copy-done.11, bf16[1,4096,384]{2,1,0:T(8,128)(2,1)S(1)} %copy-done.5), kind=kOutput, calls=%fused_computation.15 | convolution fusion | flops 3221225472 | bytes 13107200 | tf_op jit(solution)/shard_map/dot_general | solution.py:51
  267.0 7.2 %multiply_convert_fusion.1 = (bf16[1024,384]{1,0:T(8,128)(2,1)}, bf16[1024,384]{1,0:T(8,128)(2,1)}, bf16[1024,384]{1,0:T(8,128)(2,1)S(1)}) fusion(f32[1024,384]{1,0:T(8,128)} %fusion.5, f32[1024,384]{1,0:T(8,128)S(1)} %fusion.4, bf16[1,384,4096]{2,1,0:T(8,128)(2,1)S(1)} %copy-done, bf16[2,128,8,4096]{3,2,1,0:T(8,128)(2,1)S(1)} %copy-done.11), kind=kOutput, calls=%fused_computation.30 | convolution fusion | flops 3227123712 | bytes 17039360 | tf_op jit(solution)/shard_map/dot_general | solution.py:58
  274.2 0.9 copy-done.12
  275.1 6.7 %convert_bitcast_fusion = bf16[1,128,8,4096]{3,1,2,0:T(8,128)(2,1)} fusion(bf16[1,384,4096]{2,1,0:T(8,128)(2,1)S(1)} %copy-done, bf16[128,8,384]{2,1,0:T(8,128)(2,1)S(1)} %bitcast.73), kind=kOutput, calls=%fused_computation.8 | convolution fusion | flops 3225419776 | bytes 12320768 | tf_op jit(solution)/shard_map/dot_general | solution.py:56
  281.8 0.0 reduce-scatter.3.cloned.1.call-update
  281.8 0.0 reduce-scatter.5.cloned.1.call-start
  281.8 0.0 copy-start.4
  281.9 0.0 copy-start.6
  281.9 14.2 %fusion.13 = f32[1024,4096]{1,0:T(8,128)} fusion(bf16[1024,384]{1,0:T(8,128)(2,1)} %get-tuple-element.27, bf16[1,4096,384]{2,1,0:T(8,128)(2,1)} %param.11), kind=kOutput, calls=%fused_computation.27 | convolution fusion | flops 3221225472 | bytes 20709376 | tf_op jit(solution)/shard_map/dot_general | solution.py:68
  296.1 12.5 %fusion = bf16[1,128,8,4096]{3,2,0,1:T(8,128)(2,1)} fusion(f32[1024,4096]{1,0:T(8,128)} %fusion.13, bf16[1024,384]{1,0:T(8,128)(2,1)S(1)} %copy-done.6, bf16[1,4096,384]{2,1,0:T(8,128)(2,1)S(1)} %copy-done.4), kind=kOutput, calls=%fused_computation.5 | convolution fusion | flops 3229614080 | bytes 29097984 | tf_op jit(solution)/shard_map/dot_general | solution.py:68
  308.6 0.0 reduce-scatter.5.cloned.1.call-update
  308.7 0.0 reduce-scatter.3.cloned.1.call-done
  308.7 6.5 %copy.72 = bf16[1,64,8,4096]{3,2,0,1:T(8,128)(2,1)} copy(bf16[1,64,8,4096]{3,1,2,0:T(8,128)(2,1)} %reduce-scatter.3.cloned.1.call-done) | data formatting | bytes 8388608 | tf_op jit(solution)/shard_map/reduce_scatter | solution.py:14
  315.2 10.7 %all-to-all-start.1 = ((bf16[1,64,8,4096]{3,2,0,1:T(8,128)(2,1)}), bf16[1,64,8,4096]{3,2,0,1:T(8,128)(2,1)}, u32[]{:S(2)}, u32[]{:S(2)}) async-start(bf16[1,64,8,4096]{3,2,0,1:T(8,128)(2,1)} %copy.72), calls=%async_computation.2 | async-start | bytes 8388608 | tf_op jit(solution)/shard_map/all_to_all | solution.py:15
  325.9 1.6 convert_element_type.76
  327.5 2.3 reduce-scatter.5.cloned.1.call-done
  329.8 50.1 %all-to-all-done.1 = bf16[1,64,8,4096]{3,2,0,1:T(8,128)(2,1)} async-done(((bf16[1,64,8,4096]{3,2,0,1:T(8,128)(2,1)}), bf16[1,64,8,4096]{3,2,0,1:T(8,128)(2,1)}, u32[]{:S(2)}, u32[]{:S(2)}) %all-to-all-start.1) | async-done | bytes 4194336 | tf_op jit(solution)/shard_map/all_to_all | solution.py:15
  379.9 10.4 %all-to-all-start.2 = ((bf16[1,64,8,4096]{3,2,0,1:T(8,128)(2,1)}), bf16[1,64,8,4096]{3,2,0,1:T(8,128)(2,1)}, u32[]{:S(2)}, u32[]{:S(2)}) async-start(bf16[1,64,8,4096]{3,2,0,1:T(8,128)(2,1)} %reduce-scatter.5.cloned.1.call-done), calls=%async_computation.4 | async-start | bytes 8388608 | tf_op jit(solution)/shard_map/all_to_all | solution.py:15
  390.3 0.0 copy-start.7
  390.4 8.7 %fusion.8 = bf16[1,384,4096]{2,1,0:T(8,128)(2,1)} fusion(bf16[1024,384]{1,0:T(8,128)(2,1)S(1)} %copy-done.13, bf16[2,128,8,4096]{3,2,1,0:T(8,128)(2,1)} %all-gather.2.cloned.1.call-done), kind=kOutput, calls=%fused_computation.18 | convolution fusion | flops 3222798336 | bytes 12320768 | tf_op jit(solution)/shard_map/dot_general | solution.py:65
  399.1 9.5 %fusion.7 = bf16[1,4096,384]{2,1,0:T(8,128)(2,1)} fusion(bf16[1024,384]{1,0:T(8,128)(2,1)S(1)} %copy-done.7, bf16[2,128,8,4096]{3,2,1,0:T(8,128)(2,1)} %all-gather.2.cloned.1.call-done), kind=kOutput, calls=%fused_computation.17 | convolution fusion | flops 3222798336 | bytes 12320768 | tf_op jit(solution)/shard_map/dot_general | solution.py:64
  408.6 6.3 %fusion.6 = bf16[1,4096,384]{2,1,0:T(8,128)(2,1)} fusion(bf16[1024,384]{1,0:T(8,128)(2,1)S(1)} %copy-done.8, bf16[2,128,8,4096]{3,2,1,0:T(8,128)(2,1)S(1)} %bitcast.72), kind=kOutput, calls=%fused_computation.16 | convolution fusion | flops 3222798336 | bytes 12320768 | tf_op jit(solution)/shard_map/dot_general | solution.py:63
  414.9 6.6 %gather_fusion = bf16[256,4096]{1,0:T(8,128)(2,1)S(1)} fusion(bf16[512,4096]{1,0:T(8,128)(2,1)} %bitcast.11, s32[1024]{0:T(1024)S(1)} %pad_clamp_fusion), kind=kCustom, calls=%fused_computation | custom fusion | bytes 4195328 | tf_op jit(solution)/shard_map/gather | solution.py:72
  421.5 4.0 reshape.131
  425.5 10.3 %multiply_reduce_fusion = (f32[128,2]{1,0:T(8,128)S(1)}, bf16[128,4096]{1,0:T(8,128)(2,1)}) fusion(f32[128,2,4096]{2,1,0:T(2,128)} %reshape.131, f32[128,4096]{1,0:T(8,128)} %convert_element_type.76, f32[128,2]{1,0:T(8,128)S(1)} %copy.63), kind=kLoop, calls=%fused_computation.20 | loop fusion | flops 3669760 | bytes 7342080 | tf_op jit(solution)/shard_map/reduce_sum | solution.py:75
  435.8 0.6 copy.74
  436.4 5.0 %all-to-all-done.2 = bf16[1,64,8,4096]{3,2,0,1:T(8,128)(2,1)} async-done(((bf16[1,64,8,4096]{3,2,0,1:T(8,128)(2,1)}), bf16[1,64,8,4096]{3,2,0,1:T(8,128)(2,1)}, u32[]{:S(2)}, u32[]{:S(2)}) %all-to-all-start.2) | async-done | bytes 4194336 | tf_op jit(solution)/shard_map/all_to_all | solution.py:15
  441.4 8.1 %gather_fusion.1 = bf16[256,4096]{1,0:T(8,128)(2,1)} fusion(bf16[512,4096]{1,0:T(8,128)(2,1)} %bitcast.15, s32[1024]{0:T(1024)S(1)} %pad_clamp_fusion), kind=kCustom, calls=%fused_computation.1 | custom fusion | bytes 4195328 | tf_op jit(solution)/shard_map/gather | solution.py:76
  449.5 4.7 reshape.130
  454.2 7.7 %reduce_sum.41 = bf16[128,4096]{1,0:T(8,128)(2,1)} reduce(bf16[128,2,4096]{2,1,0:T(2,128)(2,1)} %reshape.130, bf16[]{:T(256)} %constant.9.clone.1), dimensions={1}, to_apply=%region_5.6 | reduce | flops 524288 | bytes 3145730 | tf_op jit(solution)/shard_map/reduce_sum | solution.py:78
  (31 shorter events, 0.1 us)
Async XLA Ops:
  7.2 259.9 %copy-start = (bf16[1,384,4096]{2,1,0:T(8,128)(2,1)S(1)}, bf16[1,384,4096]{2,1,0:T(8,128)(2,1)}, u32[]{:S(2)}) copy-start(bf16[1,384,4096]{2,1,0:T(8,128)(2,1)} %param.13) | copy-start | bytes 9437188
  7.2 244.1 %all-gather.2.cloned.1.call-start = ((), (), s32[]{:S(2)}) async-start(), calls=%async_computation.5 | async-start | bytes 25165824 | tf_op jit(solution)/shard_map/all_gather | solution.py:45
  9.3 2.2 copy-start.9
  9.3 2.5 copy-start.10
  32.2 2.9 copy-start.2
  220.9 87.7 %reduce-scatter.3.cloned.1.call-start = ((), (), s32[]{:S(2)}) async-start(), calls=%async_computation.6 | async-start | bytes 12582912 | tf_op jit(solution)/shard_map/reduce_scatter | solution.py:14
  251.3 8.4 %copy-start.5 = (bf16[1,4096,384]{2,1,0:T(8,128)(2,1)S(1)}, bf16[1,4096,384]{2,1,0:T(8,128)(2,1)}, u32[]{:S(2)}) copy-start(bf16[1,4096,384]{2,1,0:T(8,128)(2,1)} %param.11) | copy-start | bytes 9437188
  251.3 10.1 %copy-start.11 = (bf16[2,128,8,4096]{3,2,1,0:T(8,128)(2,1)S(1)}, bf16[2,128,8,4096]{3,2,1,0:T(8,128)(2,1)}, u32[]{:S(2)}) copy-start(bf16[2,128,8,4096]{3,2,1,0:T(8,128)(2,1)} %all-gather.2.cloned.1.call-done) | copy-start | bytes 50331652
  274.2 0.9 copy-start.12
  281.8 48.0 %reduce-scatter.5.cloned.1.call-start = ((), (), s32[]{:S(2)}) async-start(), calls=%async_computation.7 | async-start | bytes 12582912 | tf_op jit(solution)/shard_map/reduce_scatter | solution.py:14
  281.8 14.3 %copy-start.4 = (bf16[1,4096,384]{2,1,0:T(8,128)(2,1)S(1)}, bf16[1,4096,384]{2,1,0:T(8,128)(2,1)}, u32[]{:S(2)}) copy-start(bf16[1,4096,384]{2,1,0:T(8,128)(2,1)} %param.12) | copy-start | bytes 9437188
  281.9 14.3 %copy-start.6 = (bf16[1024,384]{1,0:T(8,128)(2,1)S(1)}, bf16[1024,384]{1,0:T(8,128)(2,1)}, u32[]{:S(2)}) copy-start(bf16[1024,384]{1,0:T(8,128)(2,1)} %get-tuple-element.26) | copy-start | bytes 2359300
  315.2 10.7 %copy-start.3 = (bf16[128,4096]{1,0:T(8,128)(2,1)S(1)}, bf16[128,4096]{1,0:T(8,128)(2,1)}, u32[]{:S(2)}) copy-start(bf16[128,4096]{1,0:T(8,128)(2,1)} %param.8) | copy-start | bytes 3145732
  315.2 64.7 %all-to-all-start.1 = ((bf16[1,64,8,4096]{3,2,0,1:T(8,128)(2,1)}), bf16[1,64,8,4096]{3,2,0,1:T(8,128)(2,1)}, u32[]{:S(2)}, u32[]{:S(2)}) async-start(bf16[1,64,8,4096]{3,2,0,1:T(8,128)(2,1)} %copy.72), calls=%async_computation.2 | async-start | bytes 8388608 | tf_op jit(solution)/shard_map/all_to_all | solution.py:15
  327.5 62.8 %copy-start.13 = (bf16[1024,384]{1,0:T(8,128)(2,1)S(1)}, bf16[1024,384]{1,0:T(8,128)(2,1)}, u32[]{:S(2)}) copy-start(bf16[1024,384]{1,0:T(8,128)(2,1)} %copy-done.12) | copy-start | bytes 2359300
  379.9 61.5 %all-to-all-start.2 = ((bf16[1,64,8,4096]{3,2,0,1:T(8,128)(2,1)}), bf16[1,64,8,4096]{3,2,0,1:T(8,128)(2,1)}, u32[]{:S(2)}, u32[]{:S(2)}) async-start(bf16[1,64,8,4096]{3,2,0,1:T(8,128)(2,1)} %reduce-scatter.5.cloned.1.call-done), calls=%async_computation.4 | async-start | bytes 8388608 | tf_op jit(solution)/shard_map/all_to_all | solution.py:15
  390.3 8.7 %copy-start.7 = (bf16[1024,384]{1,0:T(8,128)(2,1)S(1)}, bf16[1024,384]{1,0:T(8,128)(2,1)}, u32[]{:S(2)}) copy-start(bf16[1024,384]{1,0:T(8,128)(2,1)} %get-tuple-element.26) | copy-start | bytes 2359300
  390.3 18.2 %slice-start = ((s8[16777216]{0:T(1024)(128)(4,1)}), s8[4194304]{0:T(1024)(128)(4,1)S(1)}, s32[]{:S(2)}) async-start(s8[16777216]{0:T(1024)(128)(4,1)} %bitcast.71), calls=%async_computation.8 | async-start | bytes 8388608
  390.4 18.2 %slice-start.1 = ((s8[16777216]{0:T(1024)(128)(4,1)}), s8[4194304]{0:T(1024)(128)(4,1)S(1)}, s32[]{:S(2)}) async-start(s8[16777216]{0:T(1024)(128)(4,1)} %bitcast.71), calls=%async_computation.9 | async-start | bytes 8388608
  399.0 9.5 %copy-start.8 = (bf16[1024,384]{1,0:T(8,128)(2,1)S(1)}, bf16[1024,384]{1,0:T(8,128)(2,1)}, u32[]{:S(2)}) copy-start(bf16[1024,384]{1,0:T(8,128)(2,1)} %get-tuple-element.27) | copy-start | bytes 2359300
  399.0 9.5 %slice-start.2 = ((s8[16777216]{0:T(1024)(128)(4,1)}), s8[4194304]{0:T(1024)(128)(4,1)S(1)}, s32[]{:S(2)}) async-start(s8[16777216]{0:T(1024)(128)(4,1)} %bitcast.71), calls=%async_computation.10 | async-start | bytes 8388608
  399.0 9.5 %slice-start.3 = ((s8[16777216]{0:T(1024)(128)(4,1)}), s8[4194304]{0:T(1024)(128)(4,1)S(1)}, s32[]{:S(2)}) async-start(s8[16777216]{0:T(1024)(128)(4,1)} %bitcast.71), calls=%async_computation.11 | async-start | bytes 8388608
  441.4 20.5 %copy-start.1 = (bf16[1,384,4096]{2,1,0:T(8,128)(2,1)S(1)}, bf16[1,384,4096]{2,1,0:T(8,128)(2,1)}, u32[]{:S(2)}) copy-start(bf16[1,384,4096]{2,1,0:T(8,128)(2,1)} %param.13) | copy-start | bytes 9437188
Sparse Core Ops, SparseCore 0:
  221.1 30.2 all-gather.1
  281.9 20.9 reduce-scatter.2
  308.8 20.9 reduce-scatter.4
where the time goes:
time: 478 us; the launch traced here: 469 us
  local copies, waits for them, and re-layouts  132 us (28%)
  blocking collectives  108 us (23%)
  waiting for transfers between devices  87.8 us (18%)
  matrix products  79.3 us (17%)
  other arithmetic  26.3 us (6%)
  starting transfers between devices  21.3 us (4%)
  between operations  14.5 us (3%)
    all_to_all x1, blocking collectives, on_device(): lax.all_to_all(outgoing, 'ep', split_axis=1, concat_axis=1, tiled=True)  108 us
    all_to_all x2, waiting for transfers between devices, give_back(): return lax.all_to_all(summed, 'ep', split_axis=1, concat_axis=1, tiled=True)  55.1 us
    scatter x1, local copies, waits for them, and re-layouts, on_device(): outgoing = outgoing.at[:, target_row].set(jnp.stack([copied, scaled_grads]))  34.6 us
    all_gather x1, waiting for transfers between devices, on_device(): arrived = lax.all_gather(arrived, 'tp', axis=1, tiled=True)  30.3 us
    all_to_all x2, starting transfers between devices, give_back(): return lax.all_to_all(summed, 'ep', split_axis=1, concat_axis=1, tiled=True)  21.2 us
    reshape x1, local copies, waits for them, and re-layouts, on_device(): outgoing = outgoing.reshape(2, ep_size, capacity, model_width)  16.2 us
    dot_general x1, matrix products, on_device(): jnp.dot(d_gate, gate_mat.T, preferred_element_type=jnp.float32)  14.2 us
    another operation x2, local copies, waits for them, and re-layouts, on_device(): outgoing = outgoing.at[:, target_row].set(jnp.stack([copied, scaled_grads]))  12.7 us
  transfers between devices with their start and end apart: 5, of which 4 were waited for; matrix products, arithmetic and copies ran while one was open for 17% of the time, Pallas kernels for 0%

commit v1 on v0

v1 whole, which is shorter than its diff:
```python
import functools

import jax
import jax.numpy as jnp
from jax import lax
from jax.experimental import pallas as pl
from jax.experimental.pallas import tpu as pltpu
from jax.sharding import PartitionSpec as P

TOP = 2
TOK_DEV = 128
SWAP = [(0, 1), (1, 0)]
PARTS = 4


def slot_rows(routes_ref, ep_size, capacity):
    tokens = routes_ref.shape[1]
    experts = lax.broadcasted_iota(jnp.int32, (ep_size, tokens), 0)
    named = [experts == routes_ref[k : k + 1, :] for k in range(TOP)]
    hits = functools.reduce(jnp.logical_or, named)
    ahead = lax.broadcasted_iota(jnp.int32, (tokens, tokens), 0)
    behind = lax.broadcasted_iota(jnp.int32, (tokens, tokens), 1)
    earlier = (ahead < behind).astype(jnp.bfloat16)
    prior = jnp.dot(hits.astype(jnp.bfloat16), earlier, preferred_element_type=jnp.float32)
    rows = []
    for k in range(TOP):
        slot = jnp.sum(jnp.where(named[k], prior, 0.0), axis=0, keepdims=True)
        rows.append(routes_ref[k : k + 1, :] * capacity + slot.astype(jnp.int32))
    return rows


def slot_masks(routes_ref, ep_size, capacity):
    tokens = routes_ref.shape[1]
    slots = lax.broadcasted_iota(jnp.int32, (ep_size * capacity, tokens), 0)
    return [slots == row for row in slot_rows(routes_ref, ep_size, capacity)]


def dispatch_tokens_kernel(ep_size, capacity, routes_ref, x_ref, out_ref):
    masks = slot_masks(routes_ref, ep_size, capacity)
    pick = functools.reduce(jnp.logical_or, masks).astype(jnp.bfloat16)
    out_ref[...] = jnp.dot(pick, x_ref[...], preferred_element_type=jnp.float32).astype(
        jnp.bfloat16
    )


def dispatch_grads_kernel(ep_size, capacity, routes_ref, weights_ref, x_ref, out_ref):
    masks = slot_masks(routes_ref, ep_size, capacity)
    pick = functools.reduce(jnp.logical_or, masks).astype(jnp.bfloat16)
    scale = sum(
        jnp.sum(jnp.where(masks[k], weights_ref[k : k + 1, :], 0.0), axis=1, keepdims=True)
        for k in range(TOP)
    )
    rows = jnp.dot(pick, x_ref[...], preferred_element_type=jnp.float32)
    out_ref[...] = (rows * scale).astype(jnp.bfloat16)


def split_weight(value):
    high = value.astype(jnp.bfloat16)
    low = (value - high.astype(jnp.float32)).astype(jnp.bfloat16)
    return high, low


def collect_dot(picked, rows):
    return lax.dot_general(
        picked, rows, (((0,), (0,)), ((), ())), preferred_element_type=jnp.float32
    )


def combine_outputs_kernel(
    ep_size, capacity, routes_ref, weights_ref, upstream_ref, rows_ref, mixed_ref, route_ref, acc
):
    step = pl.program_id(0)
    masks = slot_masks(routes_ref, ep_size, capacity)
    weighted = sum(
        jnp.where(masks[k], weights_ref[k : k + 1, :], 0.0) for k in range(TOP)
    )
    high, low = split_weight(weighted)
    rows = rows_ref[...]
    mixed_ref[...] = (collect_dot(high, rows) + collect_dot(low, rows)).astype(jnp.bfloat16)

    @pl.when(step == 0)
    def _():
        acc[...] = jnp.zeros_like(acc)

    acc[...] += lax.dot_general(
        rows, upstream_ref[...], (((1,), (1,)), ((), ())), preferred_element_type=jnp.float32
    )

    @pl.when(step == pl.num_programs(0) - 1)
    def _():
        for k in range(TOP):
            route_ref[k : k + 1, :] = jnp.sum(
                jnp.where(masks[k], acc[...], 0.0), axis=0, keepdims=True
            )


def combine_grads_kernel(ep_size, capacity, routes_ref, rows_ref, out_ref):
    masks = slot_masks(routes_ref, ep_size, capacity)
    pick = functools.reduce(jnp.logical_or, masks).astype(jnp.bfloat16)
    out_ref[...] = collect_dot(pick, rows_ref[...]).astype(jnp.bfloat16)


def whole(shape):
    return pl.BlockSpec(shape, lambda i: (0, 0))


def columns(rows, width):
    return pl.BlockSpec((rows, width), lambda i: (0, i))


def to_experts(rows, ep_size):
    blocks = rows.reshape(ep_size, -1, rows.shape[1])
    return lax.all_to_all(blocks, "ep", split_axis=0, concat_axis=0, tiled=True).reshape(rows.shape)


def swap(rows):
    return lax.ppermute(rows, "tp", SWAP)


def rows_dot(a, b):
    return jnp.dot(a, b, preferred_element_type=jnp.float32)


def turned_dot(a, b):
    return lax.dot_general(a, b, (((1,), (1,)), ((), ())), preferred_element_type=jnp.float32)


def weight_dot(a, b):
    return lax.dot_general(a, b, (((0,), (0,)), ((), ())), preferred_element_type=jnp.float32)


def add_up(step, acc, cols, value):
    @pl.when(step == 0)
    def _():
        acc[:, cols] = value

    @pl.when(step > 0)
    def _():
        acc[:, cols] += value


def hidden_steps(step, steps, x_ref, gate_ref, up_ref, gate_out, up_out, hidden_out):
    x = x_ref[...]
    full = slice(None)
    add_up(step, gate_out, full, rows_dot(x, gate_ref[...]))
    add_up(step, up_out, full, rows_dot(x, up_ref[...]))

    @pl.when(step == steps - 1)
    def _():
        gate_pre = gate_out[...]
        hidden_out[...] = (gate_pre * jax.nn.sigmoid(gate_pre) * up_out[...]).astype(jnp.bfloat16)


def put_parts(parts, value):
    rows = parts[0].shape[0]
    for i, part in enumerate(parts):
        part[...] = value[i * rows : (i + 1) * rows].astype(part.dtype)


def put_sums(out, value, others):
    rows = others[0].shape[0]
    for i, other in enumerate(others):
        at = slice(i * rows, (i + 1) * rows)
        out[at, :] = (value[at] + other[...].astype(jnp.float32)).astype(out.dtype)


def forward_near_kernel(steps, x_ref, gate_ref, up_ref, gate_out, up_out, hidden_out):
    hidden_steps(
        pl.program_id(0), steps, x_ref, gate_ref, up_ref, gate_out, up_out, hidden_out
    )


def forward_far_kernel(
    steps, x_ref, gate_ref, up_ref, down_ref, gate_out, up_out, hidden_out, *rows_out
):
    step = pl.program_id(0)

    @pl.when(step < steps)
    def _():
        hidden_steps(step, steps, x_ref, gate_ref, up_ref, gate_out, up_out, hidden_out)

    @pl.when(step >= steps)
    def _():
        put_parts(rows_out, rows_dot(hidden_out[...], down_ref[...]))


def forward_sum_kernel(hidden_ref, down_ref, *refs):
    put_sums(refs[-1], rows_dot(hidden_ref[...], down_ref[...]), refs[:-1])


def d_hidden_steps(step, steps, g_ref, down_ref, gate_ref, up_ref, d_gate_out, d_up_out, acc):
    add_up(step, acc, slice(None), turned_dot(g_ref[...], down_ref[...]))

    @pl.when(step == steps - 1)
    def _():
        gate_pre = gate_ref[...]
        d_hidden = acc[...]
        sigmoid_gate = jax.nn.sigmoid(gate_pre)
        d_gate_out[...] = (
            d_hidden * up_ref[...] * sigmoid_gate * (1.0 + gate_pre * (1.0 - sigmoid_gate))
        ).astype(jnp.bfloat16)
        d_up_out[...] = (d_hidden * gate_pre * sigmoid_gate).astype(jnp.bfloat16)


def backward_near_kernel(
    steps, g_ref, down_ref, gate_ref, up_ref, d_gate_out, d_up_out, acc
):
    d_hidden_steps(
        pl.program_id(0), steps, g_ref, down_ref, gate_ref, up_ref, d_gate_out, d_up_out, acc
    )


def backward_far_kernel(
    steps,
    g_ref,
    down_ref,
    gate_ref,
    up_ref,
    gate_mat_ref,
    up_mat_ref,
    d_gate_out,
    d_up_out,
    *refs,
):
    step = pl.program_id(0)
    rows_out, acc = refs[:-1], refs[-1]

    @pl.when(step < steps)
    def _():
        d_hidden_steps(
            step, steps, g_ref, down_ref, gate_ref, up_ref, d_gate_out, d_up_out, acc
        )

    @pl.when(step >= steps)
    def _():
        put_parts(
            rows_out,
            turned_dot(d_gate_out[...], gate_mat_ref[...])
            + turned_dot(d_up_out[...], up_mat_ref[...]),
        )


def backward_sum_kernel(d_gate_ref, d_up_ref, gate_mat_ref, up_mat_ref, *refs):
    value = turned_dot(d_gate_ref[...], gate_mat_ref[...]) + turned_dot(
        d_up_ref[...], up_mat_ref[...]
    )
    put_sums(refs[-1], value, refs[:-1])


def expert_calls(slots, width, units, block, params):
    steps = width // block
    bf16, f32 = jnp.bfloat16, jnp.float32
    first = lambda i: jnp.minimum(i, steps - 1)
    second = lambda i: jnp.maximum(i - steps, 0)
    same = lambda i: i
    wide = lambda rows, at: pl.BlockSpec((rows, block), lambda i: (0, at(i)))
    tall = lambda at: pl.BlockSpec((block, units), lambda i: (at(i), 0))
    held = whole((slots, units))
    parts = [wide(slots // PARTS, second)] * PARTS
    pieces = [jax.ShapeDtypeStruct((slots // PARTS, width), bf16)] * PARTS
    others = [wide(slots // PARTS, same)] * PARTS
    array = lambda columns, dtype: jax.ShapeDtypeStruct((slots, columns), dtype)
    few = pl.CostEstimate(flops=1, bytes_accessed=1, transcendentals=0)
    call = functools.partial(pl.pallas_call, compiler_params=params, cost_estimate=few)
    total = [pltpu.VMEM((slots, units), f32)]
    forward_near = call(
        functools.partial(forward_near_kernel, steps),
        grid=(steps,),
        in_specs=[wide(slots, same), tall(same), tall(same)],
        out_specs=[held, held, held],
        out_shape=[array(units, f32), array(units, f32), array(units, bf16)],
        name="forward_near",
    )
    forward_far = call(
        functools.partial(forward_far_kernel, steps),
        grid=(2 * steps,),
        in_specs=[wide(slots, first), tall(first), tall(first), wide(units, second)],
        out_specs=[held, held, held, *parts],
        out_shape=[array(units, f32), array(units, f32), array(units, bf16), *pieces],
        name="forward_far",
    )
    forward_sum = call(
        forward_sum_kernel,
        grid=(steps,),
        in_specs=[held, wide(units, same), *others],
        out_specs=wide(slots, same),
        out_shape=array(width, bf16),
        name="forward_sum",
    )
    backward_near = call(
        functools.partial(backward_near_kernel, steps),
        grid=(steps,),
        in_specs=[wide(slots, same), wide(units, same), held, held],
        out_specs=[held, held],
        out_shape=[array(units, bf16), array(units, bf16)],
        scratch_shapes=total,
        name="backward_near",
    )
    backward_far = call(
        functools.partial(backward_far_kernel, steps),
        grid=(2 * steps,),
        in_specs=[
            wide(slots, first), wide(units, first), held, held, tall(second), tall(second)
        ],
        out_specs=[held, held, *parts],
        out_shape=[array(units, bf16), array(units, bf16), *pieces],
        scratch_shapes=total,
        name="backward_far",
    )
    backward_sum = call(
        backward_sum_kernel,
        grid=(steps,),
        in_specs=[held, held, tall(same), tall(same), *others],
        out_specs=wide(slots, same),
        out_shape=array(width, bf16),
        name="backward_sum",
    )
    return forward_near, forward_far, forward_sum, backward_near, backward_far, backward_sum


def on_device(tokens, upstream, routes, route_weights, gate_weight, up_weight, down_weight):
    ep_size = lax.axis_size("ep")
    token_count, width = tokens.shape
    capacity = 2 * token_count * TOP // ep_size
    slots = ep_size * capacity
    block = min(1024, width)
    grid = (width // block,)
    routes_t = routes.T
    weights_t = route_weights.T
    small = whole((TOP, token_count))
    params = pltpu.CompilerParams(vmem_limit_bytes=40 * 1024 * 1024)
    sizes = (ep_size, capacity)

    sent_tokens = pl.pallas_call(
        functools.partial(dispatch_tokens_kernel, *sizes),
        grid=grid,
        in_specs=[small, columns(token_count, block)],
        out_specs=columns(slots, block),
        out_shape=jax.ShapeDtypeStruct((slots, width), jnp.bfloat16),
        compiler_params=params,
        name="dispatch_tokens",
    )(routes_t, tokens)
    sent_grads = pl.pallas_call(
        functools.partial(dispatch_grads_kernel, *sizes),
        grid=grid,
        in_specs=[small, small, columns(token_count, block)],
        out_specs=columns(slots, block),
        out_shape=jax.ShapeDtypeStruct((slots, width), jnp.bfloat16),
        compiler_params=params,
        name="dispatch_grads",
    )(routes_t, weights_t, upstream)

    gate_mat, up_mat, down_mat = gate_weight[0], up_weight[0], down_weight[0]

    calls = expert_calls(slots, width, gate_mat.shape[1], block, params)
    forward_near, forward_far, forward_sum, backward_near, backward_far, backward_sum = calls

    inputs = to_experts(sent_tokens, ep_size)
    inputs, sent_grads = lax.optimization_barrier((inputs, sent_grads))
    grads = to_experts(sent_grads, ep_size)
    inputs_far = swap(inputs)
    gate_near, up_near, hidden_near = forward_near(inputs, gate_mat, up_mat)
    gate_far, up_far, hidden_far, *out_far = forward_far(inputs_far, gate_mat, up_mat, down_mat)
    out = forward_sum(hidden_near, down_mat, *map(swap, out_far))
    grads, out = lax.optimization_barrier((grads, out))
    out_home = to_experts(out, ep_size)

    grads_far = swap(grads)
    d_gate_near, d_up_near = backward_near(grads, down_mat, gate_near, up_near)
    d_gate_far, d_up_far, *back_far = backward_far(
        grads_far, down_mat, gate_far, up_far, gate_mat, up_mat
    )
    back = backward_sum(d_gate_near, d_up_near, gate_mat, up_mat, *map(swap, back_far))
    out_home, back, d_up_near, hidden_near = lax.optimization_barrier(
        (out_home, back, d_up_near, hidden_near)
    )
    back_home = to_experts(back, ep_size)

    inputs_all = jnp.concatenate([inputs, inputs_far], axis=0)
    grads_all = jnp.concatenate([grads, grads_far], axis=0)
    hidden_all = jnp.concatenate([hidden_near, hidden_far], axis=0)
    d_gate_all = jnp.concatenate([d_gate_near, d_gate_far], axis=0)
    d_up_all = jnp.concatenate([d_up_near, d_up_far], axis=0)
    grad_down = weight_dot(hidden_all, grads_all).astype(jnp.bfloat16)
    grad_gate = weight_dot(inputs_all, d_gate_all).astype(jnp.bfloat16)
    grad_up = weight_dot(inputs_all, d_up_all).astype(jnp.bfloat16)

    mixed, grad_route = pl.pallas_call(
        functools.partial(combine_outputs_kernel, *sizes),
        grid=grid,
        in_specs=[small, small, columns(token_count, block), columns(slots, block)],
        out_specs=[columns(token_count, block), small],
        out_shape=[
            jax.ShapeDtypeStruct((token_count, width), jnp.bfloat16),
            jax.ShapeDtypeStruct((TOP, token_count), jnp.float32),
        ],
        scratch_shapes=[pltpu.VMEM((slots, token_count), jnp.float32)],
        compiler_params=params,
        name="combine_outputs",
    )(routes_t, weights_t, upstream, out_home)
    grad_tokens = pl.pallas_call(
        functools.partial(combine_grads_kernel, *sizes),
        grid=grid,
        in_specs=[small, columns(slots, block)],
        out_specs=columns(token_count, block),
        out_shape=jax.ShapeDtypeStruct((token_count, width), jnp.bfloat16),
        compiler_params=params,
        name="combine_grads",
    )(routes_t, back_home)
    return (mixed, grad_tokens, grad_route.T, grad_gate[None], grad_up[None], grad_down[None])


def solution(mesh):
    rows = P(("tp", "ep"), None)
    split_columns = P("ep", None, "tp")
    split_rows = P("ep", "tp", None)
    return jax.shard_map(
        on_device,
        mesh=mesh,
        in_specs=(rows, rows, rows, rows, split_columns, split_columns, split_rows),
        out_specs=(rows, rows, rows, split_columns, split_columns, split_rows),
        check_vma=False,
    )
```

time: 478 us -> 278 us (0.58); the launches traced: 469 us -> 276 us
  blocking collectives: 108 us -> 0 us
  local copies, waits for them, and re-layouts: 132 us -> 26.6 us
  Pallas kernels: 0 us -> 65 us
  matrix products: 79.3 us -> 20.8 us
  waiting for transfers between devices: 87.8 us -> 115 us
  other arithmetic: 26.3 us -> 0 us
  starting transfers between devices: 21.3 us -> 47.4 us
  between operations: 14.5 us -> 0.98 us
    all_to_all x1 -> x0, blocking collectives: 108 us -> none  [on_device(): lax.all_to_all(outgoing, 'ep', split_axis=1, concat_axis=1, tiled=True)]
    pallas_call x0 -> x10, Pallas kernels: none -> 65 us  [the longest x1 12.2 us: on_device(): forward_far(inputs_far, gate_mat, up_mat, down_mat)]
    all_to_all x2 -> x4, waiting for transfers between devices: 55.1 us -> 115 us  [to_experts(): lax.all_to_all(blocks, 'ep', split_axis=0, concat_axis=0, tiled=True)]
    dot_general x10 -> x3, matrix products: 79.3 us -> 20.8 us  [weight_dot(): lax.dot_general(a, b, (((0,), (0,)), ((), ())), preferred_element_type=jn...]
    scatter x1 -> x0, local copies, waits for them, and re-layouts: 34.6 us -> none  [on_device(): outgoing = outgoing.at[:, target_row].set(jnp.stack([copied, scaled_grads]))]
    all_gather x1 -> x0, waiting for transfers between devices: 30.3 us -> none  [on_device(): arrived = lax.all_gather(arrived, 'tp', axis=1, tiled=True)]
    all_to_all x2 -> x4, starting transfers between devices: 21.2 us -> 45.4 us  [to_experts(): lax.all_to_all(blocks, 'ep', split_axis=0, concat_axis=0, tiled=True)]
    reshape x3 -> x0, local copies, waits for them, and re-layouts: 21.1 us -> none  [the longest x1 16.2 us: on_device(): outgoing = outgoing.reshape(2, ep_size, capacity, model_width)]
  transfers between devices with their start and end apart: 5 -> 14, of which waited for: 4 -> 5; matrix products, arithmetic and copies ran while one was open for 17% -> 9% of each run, Pallas kernels for 0% -> 21%
where the time goes in v1:
time: 278 us; the launch traced here: 276 us
  waiting for transfers between devices  115 us (41%)
  Pallas kernels  65 us (23%)
  starting transfers between devices  47.4 us (17%)
  local copies, waits for them, and re-layouts  26.6 us (10%)
  matrix products  20.8 us (7%)
    all_to_all x4, waiting for transfers between devices, to_experts(): lax.all_to_all(blocks, 'ep', split_axis=0, concat_axis=0, tiled=True)  115 us
    all_to_all x4, starting transfers between devices, to_experts(): lax.all_to_all(blocks, 'ep', split_axis=0, concat_axis=0, tiled=True)  45.4 us
    unnamed x69, local copies, waits for them, and re-layouts  23.8 us
    dot_general x3, matrix products, weight_dot(): lax.dot_general(a, b, (((0,), (0,)), ((), ())), preferred_element_type=jn...  20.8 us
    pallas_call x1, Pallas kernels, on_device(): forward_far(inputs_far, gate_mat, up_mat, down_mat)  12.2 us
    pallas_call x1, Pallas kernels, on_device(): backward_far(grads_far, down_mat, gate_far, up_far, gate_mat, up_mat)  11.5 us
    pallas_call x1, Pallas kernels, on_device(): gate_near, up_near, hidden_near = forward_near(inputs, gate_mat, up_mat)  8.01 us
    pallas_call x1, Pallas kernels, on_device(): pl.pallas_call(functools.partial(combine_outputs_kernel, *sizes), grid=gr...  6.91 us
  transfers between devices with their start and end apart: 14, of which 5 were waited for; matrix products, arithmetic and copies ran while one was open for 9% of the time, Pallas kernels for 21%

profile of v1, /device:TPU:2, one launch (start us, length us, event | category | flops | bytes accessed | tf_op | source)
XLA Modules:
  0.0 276.0 jit_solution(4422018667306480735)
XLA Ops:
  0.6 1.2 copy-done.12
  1.9 0.7 copy-done.25
  2.5 2.6 dispatch_tokens.1
  5.1 2.0 copy-done.9
  7.1 11.8 %all-to-all-start = ((bf16[64,8,4096]{2,1,0:T(8,128)(2,1)}), bf16[64,8,4096]{2,1,0:T(8,128)(2,1)}, u32[]{:S(2)}, u32[]{:S(2)}) async-start(bf16[64,8,4096]{2,1,0:T(8,128)(2,1)} %bitcast.36), calls=%async_computation | async-start | bytes 8388608 | tf_op jit(solution)/shard_map/all_to_all | solution.py:113
  19.0 2.9 %dispatch_grads.1 = bf16[512,4096]{1,0:T(8,128)(2,1)S(1)} custom-call(s32[2,128]{1,0:T(2,128)S(1)} %bitcast.38, f32[2,128]{1,0:T(2,128)S(1)} %bitcast.41, bf16[128,4096]{1,0:T(8,128)(2,1)S(1)} %copy-done.10), custom_call_target="tpu_custom_call" | custom-call | tf_op jit(solution)/shard_map/dispatch_grads/pallas_call | solution.py:343
  21.9 1.9 copy-done.8
  23.9 49.1 %all-to-all-done = bf16[64,8,4096]{2,1,0:T(8,128)(2,1)} async-done(((bf16[64,8,4096]{2,1,0:T(8,128)(2,1)}), bf16[64,8,4096]{2,1,0:T(8,128)(2,1)}, u32[]{:S(2)}, u32[]{:S(2)}) %all-to-all-start) | async-done | bytes 4194336 | tf_op jit(solution)/shard_map/all_to_all | solution.py:113
  72.9 0.0 collective-permute-start
  72.9 9.3 %all-to-all-start.1 = ((bf16[64,8,4096]{2,1,0:T(8,128)(2,1)}), bf16[64,8,4096]{2,1,0:T(8,128)(2,1)}, u32[]{:S(2)}, u32[]{:S(2)}) async-start(bf16[64,8,4096]{2,1,0:T(8,128)(2,1)} %bitcast.35), calls=%async_computation.1 | async-start | bytes 8388608 | tf_op jit(solution)/shard_map/all_to_all | solution.py:113
  82.2 0.0 collective-permute-done.x_ref
  82.3 0.0 copy-start.5
  82.3 1.9 copy-done.5
  84.2 12.2 %forward_far.1 = (f32[512,384]{1,0:T(8,128)S(1)}, f32[512,384]{1,0:T(8,128)S(1)}, bf16[512,384]{1,0:T(8,128)(2,1)S(1)}, bf16[128,4096]{1,0:T(8,128)(2,1)S(1)}, b...) custom-call(bf16[512,4096]{1,0:T(8,128)(2,1)} %collective-permute-done.x_ref, ...), custom_call_target="tpu_custom_call" | custom-call | flops 1 | bytes 1 | tf_op jit(solution)/shard_map/forward_far/pallas_call | solution.py:363
  96.4 0.0 copy-start.17
  96.4 0.9 copy-done.17
  97.3 0.9 copy-done.19
  98.1 0.7 copy-done.28
  98.9 0.0 collective-permute-start.1
  98.9 0.5 collective-permute-start.2
  99.4 0.0 collective-permute-start.3
  99.4 0.5 collective-permute-start.4
  99.9 8.0 %forward_near.1 = (f32[512,384]{1,0:T(8,128)S(1)}, f32[512,384]{1,0:T(8,128)S(1)}, bf16[512,384]{1,0:T(8,128)(2,1)S(1)}) custom-call(bf16[512,4096]{1,0:T(8,128)(2,1)} %bitcast.3.x_ref, bf16[4096,384]{1,0:T(8,128)(2,1)S(1)} %bitcast.27, bf16[4096,384]{1,0:T(8,128)(2,1)S(1)} %bitcast.32), custom_call_target="tpu_custom_call" | custom-call | flops 1 | bytes 1 | tf_op jit(solution)/shard_map/forward_near/pallas_call | solution.py:362
  107.9 0.0 copy-start.13
  107.9 0.9 copy-done.13
  108.8 0.9 copy-done.15
  109.7 0.0 collective-permute-done.1.refs_0_
  109.7 0.0 collective-permute-done.4.refs_3_
  109.7 3.7 %forward_sum.1 = bf16[512,4096]{1,0:T(8,128)(2,1)S(1)} custom-call(bf16[512,384]{1,0:T(8,128)(2,1)S(1)} %get-tuple-element.60.hidden_ref, bf16[384,4096]{1,0:T(8,128)(2,1)S(1)} %bitcast.23, bf16[128,4096]{1,0:T(8,128)(2,1)S(1)} %collective-permute-done.1.refs_0_, bf16[128,4096]{1,0:T(8,128)(2,1)S(1)} %collective-permute-done.2.refs_1_, ...), custom_call_target="tpu_custom_call" | custom-call | flops 1 | bytes 1 | tf_op jit(solution)/shard_map/forward_sum/pallas_call | solution.py:364
  113.4 2.0 copy-done.7
  115.4 21.9 %all-to-all-done.1 = bf16[64,8,4096]{2,1,0:T(8,128)(2,1)} async-done(((bf16[64,8,4096]{2,1,0:T(8,128)(2,1)}), bf16[64,8,4096]{2,1,0:T(8,128)(2,1)}, u32[]{:S(2)}, u32[]{:S(2)}) %all-to-all-start.1) | async-done | bytes 4194336 | tf_op jit(solution)/shard_map/all_to_all | solution.py:113
  137.3 12.1 %all-to-all-start.2 = ((bf16[64,8,4096]{2,1,0:T(8,128)(2,1)}), bf16[64,8,4096]{2,1,0:T(8,128)(2,1)}, u32[]{:S(2)}, u32[]{:S(2)}) async-start(bf16[64,8,4096]{2,1,0:T(8,128)(2,1)} %bitcast.34), calls=%async_computation.2 | async-start | bytes 8388608 | tf_op jit(solution)/shard_map/all_to_all | solution.py:113
  149.5 0.0 collective-permute-done.5.g_ref
  149.5 0.0 copy-start.3
  149.5 1.9 copy-done.3
  151.4 1.1 copy-done.18
  152.5 1.1 copy-done.20
  153.6 11.5 %backward_far.1 = (bf16[512,384]{1,0:T(8,128)(2,1)S(1)}, bf16[512,384]{1,0:T(8,128)(2,1)S(1)}, bf16[128,4096]{1,0:T(8,128)(2,1)S(1)}, bf16[128,4096]{1,0:T(8,128...) custom-call(bf16[512,4096]{1,0:T(8,128)(2,1)} %collective-permute-done.5.g_ref, ...), custom_call_target="tpu_custom_call" | custom-call | flops 1 | bytes 1 | tf_op jit(solution)/shard_map/backward_far/pallas_call | solution.py:370
  165.1 0.0 copy-start.30
  165.1 0.7 copy-done.30
  165.9 0.7 copy-done.32
  166.6 0.5 collective-permute-start.7
  167.1 0.0 collective-permute-start.8
  167.1 0.5 collective-permute-start.9
  167.7 5.8 %backward_near.1 = (bf16[512,384]{1,0:T(8,128)(2,1)S(1)}, bf16[512,384]{1,0:T(8,128)(2,1)S(1)}) custom-call(bf16[512,4096]{1,0:T(8,128)(2,1)} %bitcast.5.g_ref, bf16[384,4096]{1,0:T(8,128)(2,1)S(1)} %bitcast.25, f32[512,384]{1,0:T(8,128)S(1)} %copy-done.14, f32[512,384]{1,0:T(8,128)S(1)} %copy-done.16), custom_call_target="tpu_custom_call" | custom-call | flops 1 | bytes 1 | tf_op jit(solution)/shard_map/backward_near/pallas_call | solution.py:369
  173.4 0.0 collective-permute-done.6.refs_0_
  173.4 0.0 collective-permute-done.7.refs_1_
  173.5 0.3 collective-permute-done.9.refs_3_
  173.8 6.5 %backward_sum.1 = bf16[512,4096]{1,0:T(8,128)(2,1)} custom-call(bf16[512,384]{1,0:T(8,128)(2,1)S(1)} %get-tuple-element.45.d_gate_ref, bf16[512,384]{1,0:T(8,128)(2,1)S(1)} %get-tuple-element.58.d_up_ref, bf16[4096,384]{1,0:T(8,128)(2,1)S(1)} %bitcast.29, bf16[4096,384]{1,0:T(8,128)(2,1)S(1)} %bitcast.33, ...), custom_call_target="tpu_custom_call" | custom-call | flops 1 | bytes 1 | tf_op jit(solution)/shard_map/backward_sum/pallas_call | solution.py:373
  180.3 0.8 copy-done.21
  181.1 0.7 copy-done.23
  181.8 22.7 %all-to-all-done.2 = bf16[64,8,4096]{2,1,0:T(8,128)(2,1)} async-done(((bf16[64,8,4096]{2,1,0:T(8,128)(2,1)}), bf16[64,8,4096]{2,1,0:T(8,128)(2,1)}, u32[]{:S(2)}, u32[]{:S(2)}) %all-to-all-start.2) | async-done | bytes 4194336 | tf_op jit(solution)/shard_map/all_to_all | solution.py:113
  204.6 12.1 %all-to-all-start.3 = ((bf16[64,8,4096]{2,1,0:T(8,128)(2,1)}), bf16[64,8,4096]{2,1,0:T(8,128)(2,1)}, u32[]{:S(2)}, u32[]{:S(2)}) async-start(bf16[64,8,4096]{2,1,0:T(8,128)(2,1)} %bitcast.43), calls=%async_computation.3 | async-start | bytes 8388608 | tf_op jit(solution)/shard_map/all_to_all | solution.py:113
  216.7 2.7 constant_dynamic-update-slice_fusion.1
  219.4 0.0 copy-start.24
  219.4 0.0 copy-start.33
  219.4 2.7 constant_dynamic-update-slice_fusion
  222.2 0.0 copy-start.11
  222.2 6.0 %fusion.7 = bf16[1,4096,384]{2,1,0:T(8,128)(2,1)} fusion(bf16[1024,4096]{1,0:T(8,128)(2,1)S(1)} %constant_dynamic-update-slice_fusion, bf16[512,384]{1,0:T(8,128)(2,1)S(1)} %copy-done.33, bf16[512,384]{1,0:T(8,128)(2,1)S(1)} %copy-done.24), kind=kOutput, calls=%fused_computation.7 | convolution fusion | flops 3224371200 | bytes 12320768 | tf_op jit(solution)/shard_map/dot_general | solution.py:129
  228.2 6.9 %combine_outputs.1 = (bf16[128,4096]{1,0:T(8,128)(2,1)}, f32[2,128]{1,0:T(2,128)}) custom-call(s32[2,128]{1,0:T(2,128)S(1)} %bitcast.39, f32[2,128]{1,0:T(2,128)S(1)} %bitcast.42, bf16[128,4096]{1,0:T(8,128)(2,1)S(1)} %copy-done.11, bf16[512,4096]{1,0:T(8,128)(2,1)} %bitcast.10.rows_ref), custom_call_target="tpu_custom_call" | custom-call | tf_op jit(solution)/shard_map/combine_outputs/pallas_call | solution.py:388
  235.2 8.7 %fusion.9 = bf16[1,384,4096]{2,1,0:T(8,128)(2,1)} fusion(bf16[512,4096]{1,0:T(8,128)(2,1)} %collective-permute-done.5.g_ref, bf16[512,4096]{1,0:T(8,128)(2,1)} %bitcast.5.g_ref, bf16[512,384]{1,0:T(8,128)(2,1)S(1)} %copy-done.29, bf16[512,384]{1,0:T(8,128)(2,1)S(1)} %get-tuple-element.60.hidden_ref), kind=kOutput, calls=%fused_computation.9 | convolution fusion | flops 3241148416 | bytes 12320768 | tf_op jit(solution)/shard_map/dot_general | solution.py:129
  243.9 6.0 %fusion.8 = bf16[1,4096,384]{2,1,0:T(8,128)(2,1)} fusion(bf16[1024,4096]{1,0:T(8,128)(2,1)S(1)} %constant_dynamic-update-slice_fusion, bf16[512,384]{1,0:T(8,128)(2,1)S(1)} %copy-done.31, bf16[512,384]{1,0:T(8,128)(2,1)S(1)} %copy-done.22), kind=kOutput, calls=%fused_computation.8 | convolution fusion | flops 3224371200 | bytes 12320768 | tf_op jit(solution)/shard_map/dot_general | solution.py:129
  249.9 21.2 %all-to-all-done.3 = bf16[64,8,4096]{2,1,0:T(8,128)(2,1)} async-done(((bf16[64,8,4096]{2,1,0:T(8,128)(2,1)}), bf16[64,8,4096]{2,1,0:T(8,128)(2,1)}, u32[]{:S(2)}, u32[]{:S(2)}) %all-to-all-start.3) | async-done | bytes 4194336 | tf_op jit(solution)/shard_map/all_to_all | solution.py:113
  271.1 4.9 %combine_grads.1 = bf16[128,4096]{1,0:T(8,128)(2,1)} custom-call(s32[2,128]{1,0:T(2,128)S(1)} %bitcast.40, bf16[512,4096]{1,0:T(8,128)(2,1)} %bitcast.12.rows_ref), custom_call_target="tpu_custom_call" | custom-call | tf_op jit(solution)/shard_map/combine_grads/pallas_call | solution.py:401
  (47 shorter events, 0.1 us)
Async XLA Ops:
  0.6 1.2 copy-start.12
  1.9 0.7 copy-start.25
  5.1 2.0 copy-start.9
  7.1 11.8 %copy-start.10 = (bf16[128,4096]{1,0:T(8,128)(2,1)S(1)}, bf16[128,4096]{1,0:T(8,128)(2,1)}, u32[]{:S(2)}) copy-start(bf16[128,4096]{1,0:T(8,128)(2,1)} %upstream_ref.1) | copy-start | bytes 3145732
  7.1 11.8 %copy-start.26 = (s32[128,2]{0,1:T(2,128)S(1)}, s32[128,2]{0,1:T(2,128)}, u32[]{:S(2)}) copy-start(s32[128,2]{0,1:T(2,128)} %param.9) | copy-start | bytes 3076
  7.1 11.8 %copy-start.27 = (f32[128,2]{0,1:T(2,128)S(1)}, f32[128,2]{0,1:T(2,128)}, u32[]{:S(2)}) copy-start(f32[128,2]{0,1:T(2,128)} %param.10) | copy-start | bytes 3076
  7.1 65.8 %all-to-all-start = ((bf16[64,8,4096]{2,1,0:T(8,128)(2,1)}), bf16[64,8,4096]{2,1,0:T(8,128)(2,1)}, u32[]{:S(2)}, u32[]{:S(2)}) async-start(bf16[64,8,4096]{2,1,0:T(8,128)(2,1)} %bitcast.36), calls=%async_computation | async-start | bytes 8388608 | tf_op jit(solution)/shard_map/all_to_all | solution.py:113
  21.9 1.9 copy-start.8
  72.9 9.3 %collective-permute-start = (bf16[512,4096]{1,0:T(8,128)(2,1)}, bf16[512,4096]{1,0:T(8,128)(2,1)}, u32[]{:S(2)}, u32[]{:S(2)}) collective-permute-start(bf16[512,4096]{1,0:T(8,128)(2,1)} %bitcast.3.x_ref), channel_id=1, source_target_pairs={{0,64},{64,0},{1,65},{65,1},{2,66},{66,2},{3,67},{67,3},{4,68},{68... | collective-permute-start | bytes 12582920 | tf_op jit(solution)/shard_map/ppermute | solution.py:117
  72.9 9.3 %copy-start.1 = (bf16[1,4096,384]{2,1,0:T(8,128)(2,1)S(1)}, bf16[1,4096,384]{2,1,0:T(8,128)(2,1)}, u32[]{:S(2)}) copy-start(bf16[1,4096,384]{2,1,0:T(8,128)(2,1)} %param.11) | copy-start | bytes 9437188
  72.9 64.4 %all-to-all-start.1 = ((bf16[64,8,4096]{2,1,0:T(8,128)(2,1)}), bf16[64,8,4096]{2,1,0:T(8,128)(2,1)}, u32[]{:S(2)}, u32[]{:S(2)}) async-start(bf16[64,8,4096]{2,1,0:T(8,128)(2,1)} %bitcast.35), calls=%async_computation.1 | async-start | bytes 8388608 | tf_op jit(solution)/shard_map/all_to_all | solution.py:113
  82.3 1.9 copy-start.5
  84.2 15.8 %copy-start.2 = (bf16[1,4096,384]{2,1,0:T(8,128)(2,1)S(1)}, bf16[1,4096,384]{2,1,0:T(8,128)(2,1)}, u32[]{:S(2)}) copy-start(bf16[1,4096,384]{2,1,0:T(8,128)(2,1)} %param.11) | copy-start | bytes 9437188
  96.4 0.9 copy-start.17
  97.3 0.9 copy-start.19
  98.1 0.7 copy-start.28
  98.9 10.8 %collective-permute-start.1 = (bf16[128,4096]{1,0:T(8,128)(2,1)S(1)}, bf16[128,4096]{1,0:T(8,128)(2,1)S(1)}, u32[]{:S(2)}, u32[]{:S(2)}) collective-permute-start(bf16[128,4096]{1,0:T(8,128)(2,1)S(1)} %get-tuple-element.37), channel_id=1, source_target_pairs={{0,64},{64,0},{1,65},{65,1},{2,66},{66,2},{3,67},{67,3},{4,68},{68... | collective-permute-start | bytes 3145736 | tf_op jit(solution)/shard_map/ppermute | solution.py:117
  98.9 10.8 %collective-permute-start.2 = (bf16[128,4096]{1,0:T(8,128)(2,1)S(1)}, bf16[128,4096]{1,0:T(8,128)(2,1)S(1)}, u32[]{:S(2)}, u32[]{:S(2)}) collective-permute-start(bf16[128,4096]{1,0:T(8,128)(2,1)S(1)} %get-tuple-element.38), channel_id=1, source_target_pairs={{0,64},{64,0},{1,65},{65,1},{2,66},{66,2},{3,67},{67,3},{4,68},{68... | collective-permute-start | bytes 3145736 | tf_op jit(solution)/shard_map/ppermute | solution.py:117
  99.4 10.3 %collective-permute-start.3 = (bf16[128,4096]{1,0:T(8,128)(2,1)S(1)}, bf16[128,4096]{1,0:T(8,128)(2,1)S(1)}, u32[]{:S(2)}, u32[]{:S(2)}) collective-permute-start(bf16[128,4096]{1,0:T(8,128)(2,1)S(1)} %get-tuple-element.39), channel_id=1, source_target_pairs={{0,64},{64,0},{1,65},{65,1},{2,66},{66,2},{3,67},{67,3},{4,68},{68... | collective-permute-start | bytes 3145736 | tf_op jit(solution)/shard_map/ppermute | solution.py:117
  99.4 10.3 %copy-start = (bf16[1,384,4096]{2,1,0:T(8,128)(2,1)S(1)}, bf16[1,384,4096]{2,1,0:T(8,128)(2,1)}, u32[]{:S(2)}) copy-start(bf16[1,384,4096]{2,1,0:T(8,128)(2,1)} %param.13) | copy-start | bytes 9437188
  99.4 10.3 %collective-permute-start.4 = (bf16[128,4096]{1,0:T(8,128)(2,1)S(1)}, bf16[128,4096]{1,0:T(8,128)(2,1)S(1)}, u32[]{:S(2)}, u32[]{:S(2)}) collective-permute-start(bf16[128,4096]{1,0:T(8,128)(2,1)S(1)} %get-tuple-element.40), channel_id=1, source_target_pairs={{0,64},{64,0},{1,65},{65,1},{2,66},{66,2},{3,67},{67,3},{4,68},{68... | collective-permute-start | bytes 3145736 | tf_op jit(solution)/shard_map/ppermute | solution.py:117
  107.9 0.9 copy-start.13
  108.8 0.9 copy-start.15
  113.4 2.0 copy-start.7
  137.3 12.1 %collective-permute-start.5 = (bf16[512,4096]{1,0:T(8,128)(2,1)}, bf16[512,4096]{1,0:T(8,128)(2,1)}, u32[]{:S(2)}, u32[]{:S(2)}) collective-permute-start(bf16[512,4096]{1,0:T(8,128)(2,1)} %bitcast.5.g_ref), channel_id=1, source_target_pairs={{0,64},{64,0},{1,65},{65,1},{2,66},{66,2},{3,67},{67,3},{4,68},{68... | collective-permute-start | bytes 12582920 | tf_op jit(solution)/shard_map/ppermute | solution.py:117
  137.3 67.2 %all-to-all-start.2 = ((bf16[64,8,4096]{2,1,0:T(8,128)(2,1)}), bf16[64,8,4096]{2,1,0:T(8,128)(2,1)}, u32[]{:S(2)}, u32[]{:S(2)}) async-start(bf16[64,8,4096]{2,1,0:T(8,128)(2,1)} %bitcast.34), calls=%async_computation.2 | async-start | bytes 8388608 | tf_op jit(solution)/shard_map/all_to_all | solution.py:113
  149.5 1.9 copy-start.3
  151.4 1.1 copy-start.18
  152.5 1.1 copy-start.20
  153.6 14.0 %copy-start.14 = (f32[512,384]{1,0:T(8,128)S(1)}, f32[512,384]{1,0:T(8,128)}, u32[]{:S(2)}) copy-start(f32[512,384]{1,0:T(8,128)} %copy-done.13) | copy-start | bytes 2359300
  153.6 14.0 %copy-start.16 = (f32[512,384]{1,0:T(8,128)S(1)}, f32[512,384]{1,0:T(8,128)}, u32[]{:S(2)}) copy-start(f32[512,384]{1,0:T(8,128)} %copy-done.15) | copy-start | bytes 2359300
  165.1 0.7 copy-start.30
  165.9 0.7 copy-start.32
  166.6 6.8 %collective-permute-start.6 = (bf16[128,4096]{1,0:T(8,128)(2,1)S(1)}, bf16[128,4096]{1,0:T(8,128)(2,1)S(1)}, u32[]{:S(2)}, u32[]{:S(2)}) collective-permute-start(bf16[128,4096]{1,0:T(8,128)(2,1)S(1)} %get-tuple-element.49), channel_id=1, source_target_pairs={{0,64},{64,0},{1,65},{65,1},{2,66},{66,2},{3,67},{67,3},{4,68},{68... | collective-permute-start | bytes 3145736 | tf_op jit(solution)/shard_map/ppermute | solution.py:117
  166.6 6.8 %collective-permute-start.7 = (bf16[128,4096]{1,0:T(8,128)(2,1)S(1)}, bf16[128,4096]{1,0:T(8,128)(2,1)S(1)}, u32[]{:S(2)}, u32[]{:S(2)}) collective-permute-start(bf16[128,4096]{1,0:T(8,128)(2,1)S(1)} %get-tuple-element.50), channel_id=1, source_target_pairs={{0,64},{64,0},{1,65},{65,1},{2,66},{66,2},{3,67},{67,3},{4,68},{68... | collective-permute-start | bytes 3145736 | tf_op jit(solution)/shard_map/ppermute | solution.py:117
  167.1 6.3 %collective-permute-start.8 = (bf16[128,4096]{1,0:T(8,128)(2,1)S(1)}, bf16[128,4096]{1,0:T(8,128)(2,1)S(1)}, u32[]{:S(2)}, u32[]{:S(2)}) collective-permute-start(bf16[128,4096]{1,0:T(8,128)(2,1)S(1)} %get-tuple-element.51), channel_id=1, source_target_pairs={{0,64},{64,0},{1,65},{65,1},{2,66},{66,2},{3,67},{67,3},{4,68},{68... | collective-permute-start | bytes 3145736 | tf_op jit(solution)/shard_map/ppermute | solution.py:117
  167.1 6.6 %collective-permute-start.9 = (bf16[128,4096]{1,0:T(8,128)(2,1)S(1)}, bf16[128,4096]{1,0:T(8,128)(2,1)S(1)}, u32[]{:S(2)}, u32[]{:S(2)}) collective-permute-start(bf16[128,4096]{1,0:T(8,128)(2,1)S(1)} %get-tuple-element.52), channel_id=1, source_target_pairs={{0,64},{64,0},{1,65},{65,1},{2,66},{66,2},{3,67},{67,3},{4,68},{68... | collective-permute-start | bytes 3145736 | tf_op jit(solution)/shard_map/ppermute | solution.py:117
  167.7 6.1 %copy-start.4 = (bf16[1,4096,384]{2,1,0:T(8,128)(2,1)S(1)}, bf16[1,4096,384]{2,1,0:T(8,128)(2,1)}, u32[]{:S(2)}) copy-start(bf16[1,4096,384]{2,1,0:T(8,128)(2,1)} %param.11) | copy-start | bytes 9437188
  167.7 6.1 %copy-start.6 = (bf16[1,4096,384]{2,1,0:T(8,128)(2,1)S(1)}, bf16[1,4096,384]{2,1,0:T(8,128)(2,1)}, u32[]{:S(2)}) copy-start(bf16[1,4096,384]{2,1,0:T(8,128)(2,1)} %param.12) | copy-start | bytes 9437188
  180.3 0.8 copy-start.21
  181.1 0.7 copy-start.23
  204.6 66.5 %all-to-all-start.3 = ((bf16[64,8,4096]{2,1,0:T(8,128)(2,1)}), bf16[64,8,4096]{2,1,0:T(8,128)(2,1)}, u32[]{:S(2)}, u32[]{:S(2)}) async-start(bf16[64,8,4096]{2,1,0:T(8,128)(2,1)} %bitcast.43), calls=%async_computation.3 | async-start | bytes 8388608 | tf_op jit(solution)/shard_map/all_to_all | solution.py:113
  219.4 2.8 %copy-start.24 = (bf16[512,384]{1,0:T(8,128)(2,1)S(1)}, bf16[512,384]{1,0:T(8,128)(2,1)}, u32[]{:S(2)}) copy-start(bf16[512,384]{1,0:T(8,128)(2,1)} %copy-done.23) | copy-start | bytes 1179652
  219.4 2.8 %copy-start.33 = (bf16[512,384]{1,0:T(8,128)(2,1)S(1)}, bf16[512,384]{1,0:T(8,128)(2,1)}, u32[]{:S(2)}) copy-start(bf16[512,384]{1,0:T(8,128)(2,1)} %copy-done.32) | copy-start | bytes 1179652
  222.2 6.1 %copy-start.11 = (bf16[128,4096]{1,0:T(8,128)(2,1)S(1)}, bf16[128,4096]{1,0:T(8,128)(2,1)}, u32[]{:S(2)}) copy-start(bf16[128,4096]{1,0:T(8,128)(2,1)} %upstream_ref.1) | copy-start | bytes 3145732
  228.2 6.9 %copy-start.29 = (bf16[512,384]{1,0:T(8,128)(2,1)S(1)}, bf16[512,384]{1,0:T(8,128)(2,1)}, u32[]{:S(2)}) copy-start(bf16[512,384]{1,0:T(8,128)(2,1)} %copy-done.28) | copy-start | bytes 1179652
  235.2 8.7 %copy-start.22 = (bf16[512,384]{1,0:T(8,128)(2,1)S(1)}, bf16[512,384]{1,0:T(8,128)(2,1)}, u32[]{:S(2)}) copy-start(bf16[512,384]{1,0:T(8,128)(2,1)} %copy-done.21) | copy-start | bytes 1179652
  235.2 8.7 %copy-start.31 = (bf16[512,384]{1,0:T(8,128)(2,1)S(1)}, bf16[512,384]{1,0:T(8,128)(2,1)}, u32[]{:S(2)}) copy-start(bf16[512,384]{1,0:T(8,128)(2,1)} %copy-done.30) | copy-start | bytes 1179652

commit v2 on v1

v2 whole, which is shorter than its diff:
```python
import functools

import jax
import jax.numpy as jnp
from jax import lax
from jax.experimental import pallas as pl
from jax.experimental.pallas import tpu as pltpu
from jax.sharding import PartitionSpec as P

TOP = 2
TOK_DEV = 128
SWAP = [(0, 1), (1, 0)]
FEW = pl.CostEstimate(flops=1, bytes_accessed=1, transcendentals=0)


def slot_rows(routes_ref, ep_size, capacity):
    tokens = routes_ref.shape[1]
    experts = lax.broadcasted_iota(jnp.int32, (ep_size, tokens), 0)
    named = [experts == routes_ref[k : k + 1, :] for k in range(TOP)]
    hits = functools.reduce(jnp.logical_or, named)
    ahead = lax.broadcasted_iota(jnp.int32, (tokens, tokens), 0)
    behind = lax.broadcasted_iota(jnp.int32, (tokens, tokens), 1)
    earlier = (ahead < behind).astype(jnp.bfloat16)
    prior = jnp.dot(hits.astype(jnp.bfloat16), earlier, preferred_element_type=jnp.float32)
    rows = []
    for k in range(TOP):
        slot = jnp.sum(jnp.where(named[k], prior, 0.0), axis=0, keepdims=True)
        rows.append(routes_ref[k : k + 1, :] * capacity + slot.astype(jnp.int32))
    return rows


def slot_masks(routes_ref, ep_size, capacity):
    tokens = routes_ref.shape[1]
    slots = lax.broadcasted_iota(jnp.int32, (ep_size * capacity, tokens), 0)
    return [slots == row for row in slot_rows(routes_ref, ep_size, capacity)]


def dispatch_tokens_kernel(ep_size, capacity, routes_ref, x_ref, out_ref):
    masks = slot_masks(routes_ref, ep_size, capacity)
    pick = functools.reduce(jnp.logical_or, masks).astype(jnp.bfloat16)
    out_ref[...] = jnp.dot(pick, x_ref[...], preferred_element_type=jnp.float32).astype(
        jnp.bfloat16
    )


def dispatch_grads_kernel(ep_size, capacity, routes_ref, weights_ref, x_ref, out_ref):
    masks = slot_masks(routes_ref, ep_size, capacity)
    pick = functools.reduce(jnp.logical_or, masks).astype(jnp.bfloat16)
    scale = sum(
        jnp.sum(jnp.where(masks[k], weights_ref[k : k + 1, :], 0.0), axis=1, keepdims=True)
        for k in range(TOP)
    )
    rows = jnp.dot(pick, x_ref[...], preferred_element_type=jnp.float32)
    out_ref[...] = (rows * scale).astype(jnp.bfloat16)


def split_weight(value):
    high = value.astype(jnp.bfloat16)
    low = (value - high.astype(jnp.float32)).astype(jnp.bfloat16)
    return high, low


def collect_dot(picked, rows):
    return lax.dot_general(
        picked, rows, (((0,), (0,)), ((), ())), preferred_element_type=jnp.float32
    )


def combine_outputs_kernel(
    ep_size, capacity, routes_ref, weights_ref, upstream_ref, rows_ref, mixed_ref, route_ref, acc
):
    step = pl.program_id(0)
    masks = slot_masks(routes_ref, ep_size, capacity)
    weighted = sum(
        jnp.where(masks[k], weights_ref[k : k + 1, :], 0.0) for k in range(TOP)
    )
    high, low = split_weight(weighted)
    rows = rows_ref[...]
    mixed_ref[...] = (collect_dot(high, rows) + collect_dot(low, rows)).astype(jnp.bfloat16)

    @pl.when(step == 0)
    def _():
        acc[...] = jnp.zeros_like(acc)

    acc[...] += lax.dot_general(
        rows, upstream_ref[...], (((1,), (1,)), ((), ())), preferred_element_type=jnp.float32
    )

    @pl.when(step == pl.num_programs(0) - 1)
    def _():
        for k in range(TOP):
            route_ref[k : k + 1, :] = jnp.sum(
                jnp.where(masks[k], acc[...], 0.0), axis=0, keepdims=True
            )


def combine_grads_kernel(ep_size, capacity, routes_ref, rows_ref, out_ref):
    masks = slot_masks(routes_ref, ep_size, capacity)
    pick = functools.reduce(jnp.logical_or, masks).astype(jnp.bfloat16)
    out_ref[...] = collect_dot(pick, rows_ref[...]).astype(jnp.bfloat16)


def rows_dot(a, b):
    return jnp.dot(a, b, preferred_element_type=jnp.float32)


def turned_dot(a, b):
    return lax.dot_general(a, b, (((1,), (1,)), ((), ())), preferred_element_type=jnp.float32)


def weight_dot(a, b):
    return lax.dot_general(a, b, (((0,), (0,)), ((), ())), preferred_element_type=jnp.float32)


def add_up(first, acc, value):
    @pl.when(first)
    def _():
        acc[...] = value

    @pl.when(jnp.logical_not(first))
    def _():
        acc[...] += value


def beside(*refs):
    return jnp.concatenate([ref[...] for ref in refs], axis=1)


def stacked(*refs):
    return jnp.concatenate([ref[...] for ref in refs], axis=0)


def forward_kernel(
    steps,
    x_ref,
    gate_a,
    gate_b,
    up_a,
    up_b,
    down_a,
    down_b,
    rows_out,
    pre,
    hidden_a,
    hidden_b,
    hidden,
):
    step = pl.program_id(0)
    units = gate_a.shape[1]
    both = 2 * units

    @pl.when(step < steps)
    def _():
        add_up(step == 0, pre, rows_dot(x_ref[...], beside(gate_a, gate_b, up_a, up_b)))

    @pl.when(step == steps - 1)
    def _():
        gate_pre = pre[:, :both]
        made = (gate_pre * jax.nn.sigmoid(gate_pre) * pre[:, both:]).astype(jnp.bfloat16)
        hidden[...] = made
        hidden_a[...] = made[:, :units]
        hidden_b[...] = made[:, units:]

    @pl.when(step >= steps)
    def _():
        rows_out[...] = rows_dot(hidden[...], stacked(down_a, down_b)).astype(jnp.bfloat16)


def backward_kernel(
    steps,
    g_ref,
    pre,
    down_a,
    down_b,
    gate_a,
    gate_b,
    up_a,
    up_b,
    rows_out,
    d_gate_a,
    d_gate_b,
    d_up_a,
    d_up_b,
    d_hidden,
    d_both,
):
    step = pl.program_id(0)
    units = gate_a.shape[1]
    both = 2 * units

    @pl.when(step < steps)
    def _():
        add_up(step == 0, d_hidden, turned_dot(g_ref[...], stacked(down_a, down_b)))

    @pl.when(step == steps - 1)
    def _():
        gate_pre = pre[:, :both]
        sigmoid_gate = jax.nn.sigmoid(gate_pre)
        d_rows = d_hidden[...]
        d_gate = (
            d_rows * pre[:, both:] * sigmoid_gate * (1.0 + gate_pre * (1.0 - sigmoid_gate))
        ).astype(jnp.bfloat16)
        d_up = (d_rows * gate_pre * sigmoid_gate).astype(jnp.bfloat16)
        d_both[:, :both] = d_gate
        d_both[:, both:] = d_up
        d_gate_a[...] = d_gate[:, :units]
        d_gate_b[...] = d_gate[:, units:]
        d_up_a[...] = d_up[:, :units]
        d_up_b[...] = d_up[:, units:]

    @pl.when(step >= steps)
    def _():
        rows_out[...] = turned_dot(d_both[...], beside(gate_a, gate_b, up_a, up_b)).astype(
            jnp.bfloat16
        )


def expert_calls(slots, width, units, block, params):
    steps = width // block
    bf16, f32 = jnp.bfloat16, jnp.float32
    first = lambda i: jnp.minimum(i, steps - 1)
    second = lambda i: jnp.maximum(i - steps, 0)
    rows = lambda at: pl.BlockSpec((slots, block), lambda i: (0, at(i)))
    wide = lambda at: pl.BlockSpec((units, block), lambda i: (0, at(i)))
    tall = lambda at: pl.BlockSpec((block, units), lambda i: (at(i), 0))
    held = whole((slots, units))
    pre = whole((slots, 4 * units))
    array = lambda columns, dtype: jax.ShapeDtypeStruct((slots, columns), dtype)
    call = functools.partial(
        pl.pallas_call, grid=(2 * steps,), compiler_params=params, cost_estimate=FEW
    )
    forward = call(
        functools.partial(forward_kernel, steps),
        in_specs=[rows(first)] + [tall(first)] * 4 + [wide(second)] * 2,
        out_specs=[rows(second), pre, held, held],
        out_shape=[array(width, bf16), array(4 * units, f32)] + [array(units, bf16)] * 2,
        scratch_shapes=[pltpu.VMEM((slots, 2 * units), bf16)],
        name="forward",
    )
    backward = call(
        functools.partial(backward_kernel, steps),
        in_specs=[rows(first), pre] + [wide(first)] * 2 + [tall(second)] * 4,
        out_specs=[rows(second)] + [held] * 4,
        out_shape=[array(width, bf16)] + [array(units, bf16)] * 4,
        scratch_shapes=[
            pltpu.VMEM((slots, 2 * units), f32), pltpu.VMEM((slots, 4 * units), bf16)
        ],
        name="backward",
    )
    return forward, backward


def gate_up_kernel(x_near, x_far, d_gate_near, d_gate_far, d_up_near, d_up_far, gate_out, up_out):
    units = d_gate_near.shape[1]
    total = weight_dot(x_near[...], beside(d_gate_near, d_up_near)) + weight_dot(
        x_far[...], beside(d_gate_far, d_up_far)
    )
    gate_out[...] = total[:, :units].astype(jnp.bfloat16)
    up_out[...] = total[:, units:].astype(jnp.bfloat16)


def down_kernel(g_near, g_far, hidden_near, hidden_far, down_out):
    down_out[...] = (
        weight_dot(hidden_near[...], g_near[...]) + weight_dot(hidden_far[...], g_far[...])
    ).astype(jnp.bfloat16)


def cost(products, *arrays):
    moved = sum(a.size * a.dtype.itemsize for a in arrays)
    return pl.CostEstimate(flops=2 * products, bytes_accessed=moved, transcendentals=0)


def grads_of_gate_up(near, far, d_gate, d_up, block, params):
    slots, width = near.shape
    units = d_gate[0].shape[1]
    held = whole((slots, units))
    tall = pl.BlockSpec((block, units), lambda i: (i, 0))
    rows = pl.BlockSpec((slots, block), lambda i: (0, i))
    return pl.pallas_call(
        gate_up_kernel,
        grid=(width // block,),
        in_specs=[rows, rows] + [held] * 4,
        out_specs=[tall, tall],
        out_shape=[jax.ShapeDtypeStruct((width, units), jnp.bfloat16)] * 2,
        compiler_params=params,
        cost_estimate=cost(4 * slots * width * units, near, far),
        name="grad_gate_up",
    )(near, far, *d_gate, *d_up)


def grads_of_down(near, far, hidden, block, params):
    slots, width = near.shape
    units = hidden[0].shape[1]
    held = whole((slots, units))
    rows = pl.BlockSpec((slots, block), lambda i: (0, i))
    return pl.pallas_call(
        down_kernel,
        grid=(width // block,),
        in_specs=[rows, rows, held, held],
        out_specs=pl.BlockSpec((units, block), lambda i: (0, i)),
        out_shape=jax.ShapeDtypeStruct((units, width), jnp.bfloat16),
        compiler_params=params,
        cost_estimate=cost(2 * slots * width * units, near, far),
        name="grad_down",
    )(near, far, *hidden)


def whole(shape):
    return pl.BlockSpec(shape, lambda i: (0, 0))


def columns(rows, width):
    return pl.BlockSpec((rows, width), lambda i: (0, i))


def to_experts(rows, ep_size):
    blocks = rows.reshape(ep_size, -1, rows.shape[1])
    return lax.all_to_all(blocks, "ep", split_axis=0, concat_axis=0, tiled=True).reshape(rows.shape)


def swap(rows):
    return lax.ppermute(rows, "tp", SWAP)


def on_device(tokens, upstream, routes, route_weights, gate_weight, up_weight, down_weight):
    ep_size = lax.axis_size("ep")
    token_count, width = tokens.shape
    capacity = 2 * token_count * TOP // ep_size
    slots = ep_size * capacity
    block = min(1024, width // 2)
    grid = (width // block,)
    routes_t = routes.T
    weights_t = route_weights.T
    small = whole((TOP, token_count))
    params = pltpu.CompilerParams(vmem_limit_bytes=56 * 1024 * 1024)
    sizes = (ep_size, capacity)

    sent_tokens = pl.pallas_call(
        functools.partial(dispatch_tokens_kernel, *sizes),
        grid=grid,
        in_specs=[small, columns(token_count, block)],
        out_specs=columns(slots, block),
        out_shape=jax.ShapeDtypeStruct((slots, width), jnp.bfloat16),
        compiler_params=params,
        name="dispatch_tokens",
    )(routes_t, tokens)
    sent_grads = pl.pallas_call(
        functools.partial(dispatch_grads_kernel, *sizes),
        grid=grid,
        in_specs=[small, small, columns(token_count, block)],
        out_specs=columns(slots, block),
        out_shape=jax.ShapeDtypeStruct((slots, width), jnp.bfloat16),
        compiler_params=params,
        name="dispatch_grads",
    )(routes_t, weights_t, upstream)

    gate_mat, up_mat, down_mat = gate_weight[0], up_weight[0], down_weight[0]
    gate = (gate_mat, swap(gate_mat))
    up = (up_mat, swap(up_mat))
    down = (down_mat, swap(down_mat))
    forward, backward = expert_calls(slots, width, gate_mat.shape[1], block, params)

    inputs = to_experts(sent_tokens, ep_size)
    inputs, sent_grads = lax.optimization_barrier((inputs, sent_grads))
    grads = to_experts(sent_grads, ep_size)
    out, pre, hidden_a, hidden_b = forward(inputs, *gate, *up, *down)
    grads, out = lax.optimization_barrier((grads, out))
    out_home = to_experts(out, ep_size)
    back, d_gate_a, d_gate_b, d_up_a, d_up_b = backward(grads, pre, *down, *gate, *up)
    out_home, back, d_up_a, d_gate_a, hidden_a = lax.optimization_barrier(
        (out_home, back, d_up_a, d_gate_a, hidden_a)
    )
    back_home = to_experts(back, ep_size)

    grad_gate, grad_up = grads_of_gate_up(
        inputs, swap(inputs), (d_gate_a, swap(d_gate_b)), (d_up_a, swap(d_up_b)), block, params
    )
    grad_down = grads_of_down(grads, swap(grads), (hidden_a, swap(hidden_b)), block, params)
    mixed, grad_route = pl.pallas_call(
        functools.partial(combine_outputs_kernel, *sizes),
        grid=grid,
        in_specs=[small, small, columns(token_count, block), columns(slots, block)],
        out_specs=[columns(token_count, block), small],
        out_shape=[
            jax.ShapeDtypeStruct((token_count, width), jnp.bfloat16),
            jax.ShapeDtypeStruct((TOP, token_count), jnp.float32),
        ],
        scratch_shapes=[pltpu.VMEM((slots, token_count), jnp.float32)],
        compiler_params=params,
        cost_estimate=cost(3 * token_count * slots * width, upstream, out_home),
        name="combine_outputs",
    )(routes_t, weights_t, upstream, out_home)
    grad_tokens = pl.pallas_call(
        functools.partial(combine_grads_kernel, *sizes),
        grid=grid,
        in_specs=[small, columns(slots, block)],
        out_specs=columns(token_count, block),
        out_shape=jax.ShapeDtypeStruct((token_count, width), jnp.bfloat16),
        compiler_params=params,
        name="combine_grads",
    )(routes_t, back_home)
    return (mixed, grad_tokens, grad_route.T, grad_gate[None], grad_up[None], grad_down[None])


def solution(mesh):
    rows = P(("tp", "ep"), None)
    split_columns = P("ep", None, "tp")
    split_rows = P("ep", "tp", None)
    return jax.shard_map(
        on_device,
        mesh=mesh,
        in_specs=(rows, rows, rows, rows, split_columns, split_columns, split_rows),
        out_specs=(rows, rows, rows, split_columns, split_columns, split_rows),
        check_vma=False,
    )
```

time: 278 us -> 255 us (0.917)
  local copies, waits for them, and re-layouts: 26.6 us -> 2.27 us
  matrix products: 20.8 us -> 0 us
  waiting for transfers between devices: 115 us -> 131 us
  Pallas kernels: 65 us -> 79.5 us
  starting transfers between devices: 47.4 us -> 40.2 us
    unnamed x69 -> x16, local copies, waits for them, and re-layouts: 23.8 us -> 2.27 us
    dot_general x3 -> x0, matrix products: 20.8 us -> none  [weight_dot(): lax.dot_general(a, b, (((0,), (0,)), ((), ())), preferred_element_type=jn...]
    ppermute x10 -> x8, waiting for transfers between devices: 0.34 us -> 14.4 us  [swap(): return lax.ppermute(rows, 'tp', SWAP)]
    pallas_call x6 -> x4, Pallas kernels: 47.7 us -> 57.1 us  [the longest x1 19.5 us: on_device(): backward(grads, pre, *down, *gate, *up)]
    all_to_all x4, starting transfers between devices: 45.4 us -> 38.1 us  [to_experts(): lax.all_to_all(blocks, 'ep', split_axis=0, concat_axis=0, tiled=True)]
  transfers between devices with their start and end apart: 14 -> 12, of which waited for: 5 -> 7; matrix products, arithmetic and copies ran while one was open for 9% -> 0% of each run, Pallas kernels for 21% -> 27%
where the time goes in v2:
time: 255 us; the launch traced here: 253 us
  waiting for transfers between devices  131 us (51%)
  Pallas kernels  79.5 us (31%)
  starting transfers between devices  40.2 us (16%)
    all_to_all x4, waiting for transfers between devices, to_experts(): lax.all_to_all(blocks, 'ep', split_axis=0, concat_axis=0, tiled=True)  116 us
    all_to_all x4, starting transfers between devices, to_experts(): lax.all_to_all(blocks, 'ep', split_axis=0, concat_axis=0, tiled=True)  38.1 us
    pallas_call x1, Pallas kernels, on_device(): backward(grads, pre, *down, *gate, *up)  19.5 us
    pallas_call x1, Pallas kernels, on_device(): out, pre, hidden_a, hidden_b = forward(inputs, *gate, *up, *down)  19 us
    ppermute x8, waiting for transfers between devices, swap(): return lax.ppermute(rows, 'tp', SWAP)  14.4 us
    pallas_call x1, Pallas kernels, grads_of_gate_up(): pl.pallas_call(gate_up_kernel, grid=(width // block,), in_specs=[rows, ro...  10.9 us
    pallas_call x1, Pallas kernels, grads_of_down(): pl.pallas_call(down_kernel, grid=(width // block,), in_specs=[rows, rows,...  7.68 us
    pallas_call x1, Pallas kernels, on_device(): pl.pallas_call(functools.partial(combine_outputs_kernel, *sizes), grid=gr...  7.02 us
  transfers between devices with their start and end apart: 12, of which 7 were waited for; matrix products, arithmetic and copies ran while one was open for 0% of the time, Pallas kernels for 27%

profile of v2, /device:TPU:2, one launch (start us, length us, event | category | flops | bytes accessed | tf_op | source)
XLA Modules:
  0.0 253.4 jit_solution(9700282182084487014)
XLA Ops:
  0.6 5.1 %dispatch_tokens.1 = bf16[512,4096]{1,0:T(8,128)(2,1)} custom-call(s32[2,128]{1,0:T(2,128)} %bitcast.31, bf16[128,4096]{1,0:T(8,128)(2,1)} %x_ref.2), custom_call_target="tpu_custom_call" | custom-call | tf_op jit(solution)/shard_map/dispatch_tokens/pallas_call | solution.py:338
  5.7 11.7 %all-to-all-start = ((bf16[64,8,4096]{2,1,0:T(8,128)(2,1)}), bf16[64,8,4096]{2,1,0:T(8,128)(2,1)}, u32[]{:S(2)}, u32[]{:S(2)}) async-start(bf16[64,8,4096]{2,1,0:T(8,128)(2,1)} %bitcast.18), calls=%async_computation | async-start | bytes 8388608 | tf_op jit(solution)/shard_map/all_to_all | solution.py:318
  17.4 5.3 %dispatch_grads.1 = bf16[512,4096]{1,0:T(8,128)(2,1)} custom-call(s32[2,128]{1,0:T(2,128)} %bitcast.32, f32[2,128]{1,0:T(2,128)} %bitcast.35, bf16[128,4096]{1,0:T(8,128)(2,1)} %upstream_ref.1), custom_call_target="tpu_custom_call" | custom-call | tf_op jit(solution)/shard_map/dispatch_grads/pallas_call | solution.py:347
  22.8 48.7 %all-to-all-done = bf16[64,8,4096]{2,1,0:T(8,128)(2,1)} async-done(((bf16[64,8,4096]{2,1,0:T(8,128)(2,1)}), bf16[64,8,4096]{2,1,0:T(8,128)(2,1)}, u32[]{:S(2)}, u32[]{:S(2)}) %all-to-all-start) | async-done | bytes 4194336 | tf_op jit(solution)/shard_map/all_to_all | solution.py:318
  71.5 0.0 copy-start
  71.5 9.3 %all-to-all-start.1 = ((bf16[64,8,4096]{2,1,0:T(8,128)(2,1)}), bf16[64,8,4096]{2,1,0:T(8,128)(2,1)}, u32[]{:S(2)}, u32[]{:S(2)}) async-start(bf16[64,8,4096]{2,1,0:T(8,128)(2,1)} %bitcast.17), calls=%async_computation.1 | async-start | bytes 8388608 | tf_op jit(solution)/shard_map/all_to_all | solution.py:318
  80.7 0.0 copy-done
  80.7 0.1 collective-permute-start
  80.8 0.5 collective-permute-start.1
  81.3 0.1 collective-permute-start.2
  81.4 8.6 %collective-permute-done.gate_b = bf16[4096,384]{1,0:T(8,128)(2,1)S(1)} collective-permute-done((bf16[4096,384]{1,0:T(8,128)(2,1)S(1)}, bf16[4096,384]{1,0:T(8,128)(2,1)S(1)}, u32[]{:S(2)}, u32[]{:S(2)}) %collective-permute-start) | collective-permute-done | bytes 3145760 | tf_op jit(solution)/shard_map/ppermute | solution.py:322
  90.0 0.0 copy-start.1
  90.1 1.3 collective-permute-done.1.up_b
  91.3 4.5 %collective-permute-done.2.down_b = bf16[384,4096]{1,0:T(8,128)(2,1)} collective-permute-done((bf16[384,4096]{1,0:T(8,128)(2,1)}, bf16[384,4096]{1,0:T(8,128)(2,1)}, u32[]{:S(2)}, u32[]{:S(2)}) %collective-permute-start.2) | collective-permute-done | bytes 3145760 | tf_op jit(solution)/shard_map/ppermute | solution.py:322
  95.8 0.0 copy-done.1
  95.8 19.0 %forward.1 = (bf16[512,4096]{1,0:T(8,128)(2,1)}, f32[512,1536]{1,0:T(8,128)}, bf16[512,384]{1,0:T(8,128)(2,1)}, bf16[512,384]{1,0:T(8,128)(2,1)}) custom-call(bf16[512,4096]{1,0:T(8,128)(2,1)} %bitcast.3.x_ref.x_near, bf16[4096,384]{1,0:T(8,128)(2,1)} %bitcast.19, bf16[4096,384]{1,0:T(8,128)(2,1)} %copy-done.1, bf16[4096,384]{1,0:T(8,128)(2,1)} %bitcast.23, ...), custom_call_target="tpu_custom_call" | custom-call | flops 1 | bytes 1 | tf_op jit(solution)/shard_map/forward/pallas_call | solution.py:366
  114.8 17.4 %all-to-all-done.1 = bf16[64,8,4096]{2,1,0:T(8,128)(2,1)} async-done(((bf16[64,8,4096]{2,1,0:T(8,128)(2,1)}), bf16[64,8,4096]{2,1,0:T(8,128)(2,1)}, u32[]{:S(2)}, u32[]{:S(2)}) %all-to-all-start.1) | async-done | bytes 4194336 | tf_op jit(solution)/shard_map/all_to_all | solution.py:318
  132.2 10.8 %all-to-all-start.2 = ((bf16[64,8,4096]{2,1,0:T(8,128)(2,1)}), bf16[64,8,4096]{2,1,0:T(8,128)(2,1)}, u32[]{:S(2)}, u32[]{:S(2)}) async-start(bf16[64,8,4096]{2,1,0:T(8,128)(2,1)} %bitcast.29), calls=%async_computation.2 | async-start | bytes 8388608 | tf_op jit(solution)/shard_map/all_to_all | solution.py:318
  143.0 0.1 collective-permute-start.3
  143.1 0.5 collective-permute-start.6
  143.6 19.5 %backward.1 = (bf16[512,4096]{1,0:T(8,128)(2,1)}, bf16[512,384]{1,0:T(8,128)(2,1)}, bf16[512,384]{1,0:T(8,128)(2,1)}, bf16[512,384]{1,0:T(8,128)(2,1)}, bf16[512,384]{1,0:T(8,128)(2,1)}) custom-call(bf16[512,4096]{1,0:T(8,128)(2,1)} %bitcast.5.g_ref.g_near, f32[512,1536]{1,0:T(8,128)} %get-tuple-element.33.pre, bf16[384,4096]{1,0:T(8,128)(2,1)} %bitcast.27, ...), custom_call_target="tpu_custom_call" | custom-call | flops 1 | bytes 1 | tf_op jit(solution)/shard_map/backward/pallas_call | solution.py:369
  163.1 30.2 %all-to-all-done.2 = bf16[64,8,4096]{2,1,0:T(8,128)(2,1)} async-done(((bf16[64,8,4096]{2,1,0:T(8,128)(2,1)}), bf16[64,8,4096]{2,1,0:T(8,128)(2,1)}, u32[]{:S(2)}, u32[]{:S(2)}) %all-to-all-start.2) | async-done | bytes 4194336 | tf_op jit(solution)/shard_map/all_to_all | solution.py:318
  193.3 0.0 copy-start.5
  193.3 0.0 copy-start.4
  193.3 0.0 copy-start.3
  193.3 6.4 %all-to-all-start.3 = ((bf16[64,8,4096]{2,1,0:T(8,128)(2,1)}), bf16[64,8,4096]{2,1,0:T(8,128)(2,1)}, u32[]{:S(2)}, u32[]{:S(2)}) async-start(bf16[64,8,4096]{2,1,0:T(8,128)(2,1)} %bitcast.28), calls=%async_computation.3 | async-start | bytes 8388608 | tf_op jit(solution)/shard_map/all_to_all | solution.py:318
  199.7 0.0 copy-done.5
  199.7 0.3 collective-permute-start.4
  200.0 0.0 copy-done.4
  200.0 0.5 collective-permute-start.5
  200.5 0.0 copy-done.3
  200.5 0.1 collective-permute-start.7
  200.6 7.0 %combine_outputs.1 = (bf16[128,4096]{1,0:T(8,128)(2,1)}, f32[2,128]{1,0:T(2,128)}) custom-call(s32[2,128]{1,0:T(2,128)} %bitcast.33, f32[2,128]{1,0:T(2,128)} %bitcast.36, bf16[128,4096]{1,0:T(8,128)(2,1)} %upstream_ref.1, bf16[512,4096]{1,0:T(8,128)(2,1)} %bitcast.10.rows_ref), custom_call_target="tpu_custom_call" | custom-call | flops 1610612736 | bytes 5242880 | tf_op jit(solution)/shard_map/combine_outputs/pallas_call | solution.py:379
  207.6 0.0 collective-permute-done.3.x_far
  207.6 0.0 collective-permute-done.4.d_gate_far
  207.6 0.0 copy-start.6
  207.6 0.0 collective-permute-done.5.d_up_far
  207.6 0.7 copy-done.6
  208.4 0.0 copy-start.7
  208.4 0.8 copy-done.7
  209.2 10.9 %grad_gate_up.1 = (bf16[4096,384]{1,0:T(8,128)(2,1)}, bf16[4096,384]{1,0:T(8,128)(2,1)}) custom-call(bf16[512,4096]{1,0:T(8,128)(2,1)} %bitcast.3.x_ref.x_near, bf16[512,4096]{1,0:T(8,128)(2,1)} %collective-permute-done.3.x_far, bf16[512,384]{1,0:T(8,128)(2,1)} %get-tuple-element.42.d_gate_near, bf16[512,384]{1,0:T(8,128)(2,1)} %copy-done.6, ...), custom_call_target="tpu_custom_call" | custom-call | flops 6442450944 | bytes 8388608 | tf_op jit(solution)/shard_map/grad_gate_up/pallas_call | solution.py:279
  220.1 0.0 collective-permute-done.7.hidden_far
  220.1 0.0 copy-start.2
  220.1 0.0 collective-permute-done.6.g_far
  220.1 0.7 copy-done.2
  220.8 7.7 %grad_down.1 = bf16[384,4096]{1,0:T(8,128)(2,1)} custom-call(bf16[512,4096]{1,0:T(8,128)(2,1)} %bitcast.5.g_ref.g_near, bf16[512,4096]{1,0:T(8,128)(2,1)} %collective-permute-done.6.g_far, bf16[512,384]{1,0:T(8,128)(2,1)} %get-tuple-element.48.hidden_near, bf16[512,384]{1,0:T(8,128)(2,1)} %copy-done.2), custom_call_target="tpu_custom_call" | custom-call | flops 3221225472 | bytes 8388608 | tf_op jit(solution)/shard_map/grad_down/pallas_call | solution.py:296
  228.5 19.9 %all-to-all-done.3 = bf16[64,8,4096]{2,1,0:T(8,128)(2,1)} async-done(((bf16[64,8,4096]{2,1,0:T(8,128)(2,1)}), bf16[64,8,4096]{2,1,0:T(8,128)(2,1)}, u32[]{:S(2)}, u32[]{:S(2)}) %all-to-all-start.3) | async-done | bytes 4194336 | tf_op jit(solution)/shard_map/all_to_all | solution.py:318
  248.5 4.9 %combine_grads.1 = bf16[128,4096]{1,0:T(8,128)(2,1)} custom-call(s32[2,128]{1,0:T(2,128)} %bitcast.34, bf16[512,4096]{1,0:T(8,128)(2,1)} %bitcast.12.rows_ref), custom_call_target="tpu_custom_call" | custom-call | tf_op jit(solution)/shard_map/combine_grads/pallas_call | solution.py:393
Async XLA Ops:
  5.7 65.7 %all-to-all-start = ((bf16[64,8,4096]{2,1,0:T(8,128)(2,1)}), bf16[64,8,4096]{2,1,0:T(8,128)(2,1)}, u32[]{:S(2)}, u32[]{:S(2)}) async-start(bf16[64,8,4096]{2,1,0:T(8,128)(2,1)} %bitcast.18), calls=%async_computation | async-start | bytes 8388608 | tf_op jit(solution)/shard_map/all_to_all | solution.py:318
  71.5 9.3 %copy-start = (bf16[1,4096,384]{2,1,0:T(8,128)(2,1)S(1)}, bf16[1,4096,384]{2,1,0:T(8,128)(2,1)}, u32[]{:S(2)}) copy-start(bf16[1,4096,384]{2,1,0:T(8,128)(2,1)} %param.11) | copy-start | bytes 9437188
  71.5 60.7 %all-to-all-start.1 = ((bf16[64,8,4096]{2,1,0:T(8,128)(2,1)}), bf16[64,8,4096]{2,1,0:T(8,128)(2,1)}, u32[]{:S(2)}, u32[]{:S(2)}) async-start(bf16[64,8,4096]{2,1,0:T(8,128)(2,1)} %bitcast.17), calls=%async_computation.1 | async-start | bytes 8388608 | tf_op jit(solution)/shard_map/all_to_all | solution.py:318
  80.7 9.3 %collective-permute-start = (bf16[4096,384]{1,0:T(8,128)(2,1)S(1)}, bf16[4096,384]{1,0:T(8,128)(2,1)S(1)}, u32[]{:S(2)}, u32[]{:S(2)}) collective-permute-start(bf16[4096,384]{1,0:T(8,128)(2,1)S(1)} %bitcast.21), channel_id=1, source_target_pairs={{0,64},{64,0},{1,65},{65,1},{2,66},{66,2},{3,67},{67,3},{4,68},{68... | collective-permute-start | bytes 9437192 | tf_op jit(solution)/shard_map/ppermute | solution.py:322
  80.8 10.5 %collective-permute-start.1 = (bf16[4096,384]{1,0:T(8,128)(2,1)}, bf16[4096,384]{1,0:T(8,128)(2,1)}, u32[]{:S(2)}, u32[]{:S(2)}) collective-permute-start(bf16[4096,384]{1,0:T(8,128)(2,1)} %bitcast.22), channel_id=1, source_target_pairs={{0,64},{64,0},{1,65},{65,1},{2,66},{66,2},{3,67},{67,3},{4,68},{68... | collective-permute-start | bytes 9437192 | tf_op jit(solution)/shard_map/ppermute | solution.py:322
  81.3 14.5 %collective-permute-start.2 = (bf16[384,4096]{1,0:T(8,128)(2,1)}, bf16[384,4096]{1,0:T(8,128)(2,1)}, u32[]{:S(2)}, u32[]{:S(2)}) collective-permute-start(bf16[384,4096]{1,0:T(8,128)(2,1)} %bitcast.25), channel_id=1, source_target_pairs={{0,64},{64,0},{1,65},{65,1},{2,66},{66,2},{3,67},{67,3},{4,68},{68... | collective-permute-start | bytes 9437192 | tf_op jit(solution)/shard_map/ppermute | solution.py:322
  90.0 5.8 %copy-start.1 = (bf16[4096,384]{1,0:T(8,128)(2,1)}, bf16[4096,384]{1,0:T(8,128)(2,1)S(1)}, u32[]{:S(2)}) copy-start(bf16[4096,384]{1,0:T(8,128)(2,1)S(1)} %collective-permute-done.gate_b) | copy-start | bytes 9437188
  132.2 61.1 %all-to-all-start.2 = ((bf16[64,8,4096]{2,1,0:T(8,128)(2,1)}), bf16[64,8,4096]{2,1,0:T(8,128)(2,1)}, u32[]{:S(2)}, u32[]{:S(2)}) async-start(bf16[64,8,4096]{2,1,0:T(8,128)(2,1)} %bitcast.29), calls=%async_computation.2 | async-start | bytes 8388608 | tf_op jit(solution)/shard_map/all_to_all | solution.py:318
  143.0 64.6 %collective-permute-start.3 = (bf16[512,4096]{1,0:T(8,128)(2,1)}, bf16[512,4096]{1,0:T(8,128)(2,1)}, u32[]{:S(2)}, u32[]{:S(2)}) collective-permute-start(bf16[512,4096]{1,0:T(8,128)(2,1)} %bitcast.3.x_ref.x_near), channel_id=1, source_target_pairs={{0,64},{64,0},{1,65},{65,1},{2,66},{66,2},{3,67},{67,3},{4,68},{68... | collective-permute-start | bytes 12582920 | tf_op jit(solution)/shard_map/ppermute | solution.py:322
  143.1 77.0 %collective-permute-start.6 = (bf16[512,4096]{1,0:T(8,128)(2,1)}, bf16[512,4096]{1,0:T(8,128)(2,1)}, u32[]{:S(2)}, u32[]{:S(2)}) collective-permute-start(bf16[512,4096]{1,0:T(8,128)(2,1)} %bitcast.5.g_ref.g_near), channel_id=1, source_target_pairs={{0,64},{64,0},{1,65},{65,1},{2,66},{66,2},{3,67},{67,3},{4,68},{68... | collective-permute-start | bytes 12582920 | tf_op jit(solution)/shard_map/ppermute | solution.py:322
  193.3 6.4 %copy-start.5 = (bf16[512,384]{1,0:T(8,128)(2,1)S(1)}, bf16[512,384]{1,0:T(8,128)(2,1)}, u32[]{:S(2)}) copy-start(bf16[512,384]{1,0:T(8,128)(2,1)} %get-tuple-element.43) | copy-start | bytes 1179652
  193.3 6.7 %copy-start.4 = (bf16[512,384]{1,0:T(8,128)(2,1)S(1)}, bf16[512,384]{1,0:T(8,128)(2,1)}, u32[]{:S(2)}) copy-start(bf16[512,384]{1,0:T(8,128)(2,1)} %get-tuple-element.45) | copy-start | bytes 1179652
  193.3 7.2 %copy-start.3 = (bf16[512,384]{1,0:T(8,128)(2,1)S(1)}, bf16[512,384]{1,0:T(8,128)(2,1)}, u32[]{:S(2)}) copy-start(bf16[512,384]{1,0:T(8,128)(2,1)} %get-tuple-element.49) | copy-start | bytes 1179652
  193.3 55.2 %all-to-all-start.3 = ((bf16[64,8,4096]{2,1,0:T(8,128)(2,1)}), bf16[64,8,4096]{2,1,0:T(8,128)(2,1)}, u32[]{:S(2)}, u32[]{:S(2)}) async-start(bf16[64,8,4096]{2,1,0:T(8,128)(2,1)} %bitcast.28), calls=%async_computation.3 | async-start | bytes 8388608 | tf_op jit(solution)/shard_map/all_to_all | solution.py:318
  199.7 7.9 %collective-permute-start.4 = (bf16[512,384]{1,0:T(8,128)(2,1)S(1)}, bf16[512,384]{1,0:T(8,128)(2,1)S(1)}, u32[]{:S(2)}, u32[]{:S(2)}) collective-permute-start(bf16[512,384]{1,0:T(8,128)(2,1)S(1)} %copy-done.5), channel_id=1, source_target_pairs={{0,64},{64,0},{1,65},{65,1},{2,66},{66,2},{3,67},{67,3},{4,68},{68... | collective-permute-start | bytes 1179656 | tf_op jit(solution)/shard_map/ppermute | solution.py:322
  200.0 7.6 %collective-permute-start.5 = (bf16[512,384]{1,0:T(8,128)(2,1)S(1)}, bf16[512,384]{1,0:T(8,128)(2,1)S(1)}, u32[]{:S(2)}, u32[]{:S(2)}) collective-permute-start(bf16[512,384]{1,0:T(8,128)(2,1)S(1)} %copy-done.4), channel_id=1, source_target_pairs={{0,64},{64,0},{1,65},{65,1},{2,66},{66,2},{3,67},{67,3},{4,68},{68... | collective-permute-start | bytes 1179656 | tf_op jit(solution)/shard_map/ppermute | solution.py:322
  200.5 19.6 %collective-permute-start.7 = (bf16[512,384]{1,0:T(8,128)(2,1)S(1)}, bf16[512,384]{1,0:T(8,128)(2,1)S(1)}, u32[]{:S(2)}, u32[]{:S(2)}) collective-permute-start(bf16[512,384]{1,0:T(8,128)(2,1)S(1)} %copy-done.3), channel_id=1, source_target_pairs={{0,64},{64,0},{1,65},{65,1},{2,66},{66,2},{3,67},{67,3},{4,68},{68... | collective-permute-start | bytes 1179656 | tf_op jit(solution)/shard_map/ppermute | solution.py:322
  207.6 0.7 copy-start.6
  208.4 0.8 copy-start.7
  220.1 0.7 copy-start.2

commit v3 on v2

--- a/solution.py
+++ b/solution.py
@@ -328,7 +328,8 @@
     capacity = 2 * token_count * TOP // ep_size
     slots = ep_size * capacity
     block = min(1024, width // 2)
-    grid = (width // block,)
+    broad = min(2048, width // 2)
+    grid = (width // broad,)
     routes_t = routes.T
     weights_t = route_weights.T
     small = whole((TOP, token_count))
@@ -338,26 +339,30 @@
     sent_tokens = pl.pallas_call(
         functools.partial(dispatch_tokens_kernel, *sizes),
         grid=grid,
-        in_specs=[small, columns(token_count, block)],
-        out_specs=columns(slots, block),
+        in_specs=[small, columns(token_count, broad)],
+        out_specs=columns(slots, broad),
         out_shape=jax.ShapeDtypeStruct((slots, width), jnp.bfloat16),
         compiler_params=params,
         name="dispatch_tokens",
     )(routes_t, tokens)
-    sent_grads = pl.pallas_call(
-        functools.partial(dispatch_grads_kernel, *sizes),
-        grid=grid,
-        in_specs=[small, small, columns(token_count, block)],
-        out_specs=columns(slots, block),
-        out_shape=jax.ShapeDtypeStruct((slots, width), jnp.bfloat16),
-        compiler_params=params,
-        name="dispatch_grads",
-    )(routes_t, weights_t, upstream)
-
     gate_mat, up_mat, down_mat = gate_weight[0], up_weight[0], down_weight[0]
     gate = (gate_mat, swap(gate_mat))
     up = (up_mat, swap(up_mat))
     down = (down_mat, swap(down_mat))
+    gate_b, up_b, down_b, weights_late = lax.optimization_barrier(
+        (gate[1], up[1], down[1], weights_t)
+    )
+    gate, up, down = (gate_mat, gate_b), (up_mat, up_b), (down_mat, down_b)
+    sent_grads = pl.pallas_call(
+        functools.partial(dispatch_grads_kernel, *sizes),
+        grid=grid,
+        in_specs=[small, small, columns(token_count, broad)],
+        out_specs=columns(slots, broad),
+        out_shape=jax.ShapeDtypeStruct((slots, width), jnp.bfloat16),
+        compiler_params=params,
+        name="dispatch_grads",
+    )(routes_t, weights_late, upstream)
+
     forward, backward = expert_calls(slots, width, gate_mat.shape[1], block, params)
 
     inputs = to_experts(sent_tokens, ep_size)
@@ -379,8 +384,8 @@
     mixed, grad_route = pl.pallas_call(
         functools.partial(combine_outputs_kernel, *sizes),
         grid=grid,
-        in_specs=[small, small, columns(token_count, block), columns(slots, block)],
-        out_specs=[columns(token_count, block), small],
+        in_specs=[small, small, columns(token_count, broad), columns(slots, broad)],
+        out_specs=[columns(token_count, broad), small],
         out_shape=[
             jax.ShapeDtypeStruct((token_count, width), jnp.bfloat16),
             jax.ShapeDtypeStruct((TOP, token_count), jnp.float32),
@@ -393,8 +398,8 @@
     grad_tokens = pl.pallas_call(
         functools.partial(combine_grads_kernel, *sizes),
         grid=grid,
-        in_specs=[small, columns(slots, block)],
-        out_specs=columns(token_count, block),
+        in_specs=[small, columns(slots, broad)],
+        out_specs=columns(token_count, broad),
         out_shape=jax.ShapeDtypeStruct((token_count, width), jnp.bfloat16),
         compiler_params=params,
         name="combine_grads",

time: 255 us -> 251 us (0.984)
  local copies, waits for them, and re-layouts: 2.27 us -> 7.27 us
  Pallas kernels: 79.5 us -> 75.3 us
    unnamed x16 -> x20, local copies, waits for them, and re-layouts: 2.27 us -> 7.27 us
    ppermute x8, waiting for transfers between devices: 14.4 us -> 10.9 us  [swap(): return lax.ppermute(rows, 'tp', SWAP)]
  transfers between devices with their start and end apart: 12 -> 12, of which waited for: 7 -> 6; matrix products, arithmetic and copies ran while one was open for 0% -> 0% of each run, Pallas kernels for 27% -> 27%
where the time goes in v3:
time: 251 us; the launch traced here: 250 us
  waiting for transfers between devices  129 us (51%)
  Pallas kernels  75.3 us (30%)
  starting transfers between devices  38.2 us (15%)
  local copies, waits for them, and re-layouts  7.27 us (3%)
    all_to_all x4, waiting for transfers between devices, to_experts(): lax.all_to_all(blocks, 'ep', split_axis=0, concat_axis=0, tiled=True)  118 us
    all_to_all x4, starting transfers between devices, to_experts(): lax.all_to_all(blocks, 'ep', split_axis=0, concat_axis=0, tiled=True)  36.3 us
    pallas_call x1, Pallas kernels, on_device(): backward(grads, pre, *down, *gate, *up)  19.6 us
    pallas_call x1, Pallas kernels, on_device(): out, pre, hidden_a, hidden_b = forward(inputs, *gate, *up, *down)  19 us
    pallas_call x1, Pallas kernels, grads_of_gate_up(): pl.pallas_call(gate_up_kernel, grid=(width // block,), in_specs=[rows, ro...  11 us
    ppermute x8, waiting for transfers between devices, swap(): return lax.ppermute(rows, 'tp', SWAP)  10.9 us
    pallas_call x1, Pallas kernels, grads_of_down(): pl.pallas_call(down_kernel, grid=(width // block,), in_specs=[rows, rows,...  7.68 us
    unnamed x20, local copies, waits for them, and re-layouts  7.27 us
  transfers between devices with their start and end apart: 12, of which 6 were waited for; matrix products, arithmetic and copies ran while one was open for 0% of the time, Pallas kernels for 27%

profile of v3, /device:TPU:2, one launch (start us, length us, event | category | flops | bytes accessed | tf_op | source)
XLA Modules:
  0.0 250.2 jit_solution(7381605832382957686)
XLA Ops:
  0.6 4.2 %dispatch_tokens.1 = bf16[512,4096]{1,0:T(8,128)(2,1)} custom-call(s32[2,128]{1,0:T(2,128)} %bitcast.31, bf16[128,4096]{1,0:T(8,128)(2,1)} %x_ref.2), custom_call_target="tpu_custom_call" | custom-call | tf_op jit(solution)/shard_map/dispatch_tokens/pallas_call | solution.py:339
  4.8 0.0 copy-start
  4.8 11.9 %all-to-all-start = ((bf16[64,8,4096]{2,1,0:T(8,128)(2,1)}), bf16[64,8,4096]{2,1,0:T(8,128)(2,1)}, u32[]{:S(2)}, u32[]{:S(2)}) async-start(bf16[64,8,4096]{2,1,0:T(8,128)(2,1)} %bitcast.17), calls=%async_computation | async-start | bytes 8388608 | tf_op jit(solution)/shard_map/all_to_all | solution.py:318
  16.7 0.0 copy-done
  16.7 0.1 collective-permute-start
  16.8 0.5 collective-permute-start.1
  17.3 0.1 collective-permute-start.2
  17.4 8.6 %collective-permute-done.gate_b = bf16[4096,384]{1,0:T(8,128)(2,1)S(1)} collective-permute-done((bf16[4096,384]{1,0:T(8,128)(2,1)S(1)}, bf16[4096,384]{1,0:T(8,128)(2,1)S(1)}, u32[]{:S(2)}, u32[]{:S(2)}) %collective-permute-start) | collective-permute-done | bytes 3145760 | tf_op jit(solution)/shard_map/ppermute | solution.py:322
  26.1 0.0 copy-start.1
  26.1 1.7 copy-done.1
  27.7 0.0 collective-permute-done.1.up_b
  27.7 0.0 copy-start.2
  27.7 1.7 copy-done.2
  29.4 2.3 collective-permute-done.2.down_b
  31.7 0.0 copy-start.3
  31.7 1.7 copy-done.3
  33.4 4.2 %dispatch_grads.1 = bf16[512,4096]{1,0:T(8,128)(2,1)} custom-call(s32[2,128]{1,0:T(2,128)} %bitcast.32, f32[2,128]{1,0:T(2,128)} %bitcast.35, bf16[128,4096]{1,0:T(8,128)(2,1)} %upstream_ref.1), custom_call_target="tpu_custom_call" | custom-call | tf_op jit(solution)/shard_map/dispatch_grads/pallas_call | solution.py:356
  37.6 33.1 %all-to-all-done = bf16[64,8,4096]{2,1,0:T(8,128)(2,1)} async-done(((bf16[64,8,4096]{2,1,0:T(8,128)(2,1)}), bf16[64,8,4096]{2,1,0:T(8,128)(2,1)}, u32[]{:S(2)}, u32[]{:S(2)}) %all-to-all-start) | async-done | bytes 4194336 | tf_op jit(solution)/shard_map/all_to_all | solution.py:318
  70.7 9.4 %all-to-all-start.1 = ((bf16[64,8,4096]{2,1,0:T(8,128)(2,1)}), bf16[64,8,4096]{2,1,0:T(8,128)(2,1)}, u32[]{:S(2)}, u32[]{:S(2)}) async-start(bf16[64,8,4096]{2,1,0:T(8,128)(2,1)} %bitcast.18), calls=%async_computation.1 | async-start | bytes 8388608 | tf_op jit(solution)/shard_map/all_to_all | solution.py:318
  80.1 19.0 %forward.1 = (bf16[512,4096]{1,0:T(8,128)(2,1)}, f32[512,1536]{1,0:T(8,128)}, bf16[512,384]{1,0:T(8,128)(2,1)}, bf16[512,384]{1,0:T(8,128)(2,1)}) custom-call(bf16[512,4096]{1,0:T(8,128)(2,1)} %bitcast.3.x_ref.x_near, bf16[4096,384]{1,0:T(8,128)(2,1)} %bitcast.19, bf16[4096,384]{1,0:T(8,128)(2,1)} %copy-done.1, bf16[4096,384]{1,0:T(8,128)(2,1)} %bitcast.23, ...), custom_call_target="tpu_custom_call" | custom-call | flops 1 | bytes 1 | tf_op jit(solution)/shard_map/forward/pallas_call | solution.py:371
  99.2 33.0 %all-to-all-done.1 = bf16[64,8,4096]{2,1,0:T(8,128)(2,1)} async-done(((bf16[64,8,4096]{2,1,0:T(8,128)(2,1)}), bf16[64,8,4096]{2,1,0:T(8,128)(2,1)}, u32[]{:S(2)}, u32[]{:S(2)}) %all-to-all-start.1) | async-done | bytes 4194336 | tf_op jit(solution)/shard_map/all_to_all | solution.py:318
  132.1 8.9 %all-to-all-start.2 = ((bf16[64,8,4096]{2,1,0:T(8,128)(2,1)}), bf16[64,8,4096]{2,1,0:T(8,128)(2,1)}, u32[]{:S(2)}, u32[]{:S(2)}) async-start(bf16[64,8,4096]{2,1,0:T(8,128)(2,1)} %bitcast.29), calls=%async_computation.2 | async-start | bytes 8388608 | tf_op jit(solution)/shard_map/all_to_all | solution.py:318
  141.0 0.1 collective-permute-start.3
  141.1 0.5 collective-permute-start.6
  141.6 19.6 %backward.1 = (bf16[512,4096]{1,0:T(8,128)(2,1)}, bf16[512,384]{1,0:T(8,128)(2,1)}, bf16[512,384]{1,0:T(8,128)(2,1)}, bf16[512,384]{1,0:T(8,128)(2,1)}, bf16[512,384]{1,0:T(8,128)(2,1)}) custom-call(bf16[512,4096]{1,0:T(8,128)(2,1)} %bitcast.8.g_ref.g_near, f32[512,1536]{1,0:T(8,128)} %get-tuple-element.41.pre, bf16[384,4096]{1,0:T(8,128)(2,1)} %bitcast.27, ...), custom_call_target="tpu_custom_call" | custom-call | flops 1 | bytes 1 | tf_op jit(solution)/shard_map/backward/pallas_call | solution.py:374
  161.1 30.1 %all-to-all-done.2 = bf16[64,8,4096]{2,1,0:T(8,128)(2,1)} async-done(((bf16[64,8,4096]{2,1,0:T(8,128)(2,1)}), bf16[64,8,4096]{2,1,0:T(8,128)(2,1)}, u32[]{:S(2)}, u32[]{:S(2)}) %all-to-all-start.2) | async-done | bytes 4194336 | tf_op jit(solution)/shard_map/all_to_all | solution.py:318
  191.2 0.0 copy-start.7
  191.2 0.0 copy-start.6
  191.2 0.0 copy-start.5
  191.2 6.1 %all-to-all-start.3 = ((bf16[64,8,4096]{2,1,0:T(8,128)(2,1)}), bf16[64,8,4096]{2,1,0:T(8,128)(2,1)}, u32[]{:S(2)}, u32[]{:S(2)}) async-start(bf16[64,8,4096]{2,1,0:T(8,128)(2,1)} %bitcast.28), calls=%async_computation.3 | async-start | bytes 8388608 | tf_op jit(solution)/shard_map/all_to_all | solution.py:318
  197.3 0.0 copy-done.7
  197.3 0.1 collective-permute-start.4
  197.4 0.0 copy-done.6
  197.4 0.5 collective-permute-start.5
  197.9 0.0 copy-done.5
  197.9 0.1 collective-permute-start.7
  198.0 6.1 %combine_outputs.1 = (bf16[128,4096]{1,0:T(8,128)(2,1)}, f32[2,128]{1,0:T(2,128)}) custom-call(s32[2,128]{1,0:T(2,128)} %bitcast.33, f32[2,128]{1,0:T(2,128)} %bitcast.36, bf16[128,4096]{1,0:T(8,128)(2,1)} %upstream_ref.1, bf16[512,4096]{1,0:T(8,128)(2,1)} %bitcast.10.rows_ref), custom_call_target="tpu_custom_call" | custom-call | flops 1610612736 | bytes 5242880 | tf_op jit(solution)/shard_map/combine_outputs/pallas_call | solution.py:384
  204.0 0.0 collective-permute-done.3.x_far
  204.0 0.0 collective-permute-done.4.d_gate_far
  204.1 0.0 copy-start.8
  204.1 0.0 collective-permute-done.5.d_up_far
  204.1 0.7 copy-done.8
  204.8 0.0 copy-start.9
  204.8 0.8 copy-done.9
  205.6 11.0 %grad_gate_up.1 = (bf16[4096,384]{1,0:T(8,128)(2,1)}, bf16[4096,384]{1,0:T(8,128)(2,1)}) custom-call(bf16[512,4096]{1,0:T(8,128)(2,1)} %bitcast.3.x_ref.x_near, bf16[512,4096]{1,0:T(8,128)(2,1)} %collective-permute-done.3.x_far, bf16[512,384]{1,0:T(8,128)(2,1)} %get-tuple-element.50.d_gate_near, bf16[512,384]{1,0:T(8,128)(2,1)} %copy-done.8, ...), custom_call_target="tpu_custom_call" | custom-call | flops 6442450944 | bytes 8388608 | tf_op jit(solution)/shard_map/grad_gate_up/pallas_call | solution.py:279
  216.5 0.0 collective-permute-done.7.hidden_far
  216.6 0.0 copy-start.4
  216.6 0.0 collective-permute-done.6.g_far
  216.6 0.7 copy-done.4
  217.3 7.7 %grad_down.1 = bf16[384,4096]{1,0:T(8,128)(2,1)} custom-call(bf16[512,4096]{1,0:T(8,128)(2,1)} %bitcast.8.g_ref.g_near, bf16[512,4096]{1,0:T(8,128)(2,1)} %collective-permute-done.6.g_far, bf16[512,384]{1,0:T(8,128)(2,1)} %get-tuple-element.56.hidden_near, bf16[512,384]{1,0:T(8,128)(2,1)} %copy-done.4), custom_call_target="tpu_custom_call" | custom-call | flops 3221225472 | bytes 8388608 | tf_op jit(solution)/shard_map/grad_down/pallas_call | solution.py:296
  225.0 21.5 %all-to-all-done.3 = bf16[64,8,4096]{2,1,0:T(8,128)(2,1)} async-done(((bf16[64,8,4096]{2,1,0:T(8,128)(2,1)}), bf16[64,8,4096]{2,1,0:T(8,128)(2,1)}, u32[]{:S(2)}, u32[]{:S(2)}) %all-to-all-start.3) | async-done | bytes 4194336 | tf_op jit(solution)/shard_map/all_to_all | solution.py:318
  246.5 3.7 %combine_grads.1 = bf16[128,4096]{1,0:T(8,128)(2,1)} custom-call(s32[2,128]{1,0:T(2,128)} %bitcast.34, bf16[512,4096]{1,0:T(8,128)(2,1)} %bitcast.12.rows_ref), custom_call_target="tpu_custom_call" | custom-call | tf_op jit(solution)/shard_map/combine_grads/pallas_call | solution.py:398
Async XLA Ops:
  4.8 12.0 %copy-start = (bf16[1,4096,384]{2,1,0:T(8,128)(2,1)S(1)}, bf16[1,4096,384]{2,1,0:T(8,128)(2,1)}, u32[]{:S(2)}) copy-start(bf16[1,4096,384]{2,1,0:T(8,128)(2,1)} %param.11) | copy-start | bytes 9437188
  4.8 65.9 %all-to-all-start = ((bf16[64,8,4096]{2,1,0:T(8,128)(2,1)}), bf16[64,8,4096]{2,1,0:T(8,128)(2,1)}, u32[]{:S(2)}, u32[]{:S(2)}) async-start(bf16[64,8,4096]{2,1,0:T(8,128)(2,1)} %bitcast.17), calls=%async_computation | async-start | bytes 8388608 | tf_op jit(solution)/shard_map/all_to_all | solution.py:318
  16.7 9.3 %collective-permute-start = (bf16[4096,384]{1,0:T(8,128)(2,1)S(1)}, bf16[4096,384]{1,0:T(8,128)(2,1)S(1)}, u32[]{:S(2)}, u32[]{:S(2)}) collective-permute-start(bf16[4096,384]{1,0:T(8,128)(2,1)S(1)} %bitcast.21), channel_id=1, source_target_pairs={{0,64},{64,0},{1,65},{65,1},{2,66},{66,2},{3,67},{67,3},{4,68},{68... | collective-permute-start | bytes 9437192 | tf_op jit(solution)/shard_map/ppermute | solution.py:322
  16.8 10.9 %collective-permute-start.1 = (bf16[4096,384]{1,0:T(8,128)(2,1)}, bf16[4096,384]{1,0:T(8,128)(2,1)S(1)}, u32[]{:S(2)}, u32[]{:S(2)}) collective-permute-start(bf16[4096,384]{1,0:T(8,128)(2,1)} %bitcast.22), channel_id=1, source_target_pairs={{0,64},{64,0},{1,65},{65,1},{2,66},{66,2},{3,67},{67,3},{4,68},{68... | collective-permute-start | bytes 9437192 | tf_op jit(solution)/shard_map/ppermute | solution.py:322
  17.3 14.4 %collective-permute-start.2 = (bf16[384,4096]{1,0:T(8,128)(2,1)}, bf16[384,4096]{1,0:T(8,128)(2,1)S(1)}, u32[]{:S(2)}, u32[]{:S(2)}) collective-permute-start(bf16[384,4096]{1,0:T(8,128)(2,1)} %bitcast.25), channel_id=1, source_target_pairs={{0,64},{64,0},{1,65},{65,1},{2,66},{66,2},{3,67},{67,3},{4,68},{68... | collective-permute-start | bytes 9437192 | tf_op jit(solution)/shard_map/ppermute | solution.py:322
  26.1 1.7 copy-start.1
  27.7 1.7 copy-start.2
  31.7 1.7 copy-start.3
  70.7 61.4 %all-to-all-start.1 = ((bf16[64,8,4096]{2,1,0:T(8,128)(2,1)}), bf16[64,8,4096]{2,1,0:T(8,128)(2,1)}, u32[]{:S(2)}, u32[]{:S(2)}) async-start(bf16[64,8,4096]{2,1,0:T(8,128)(2,1)} %bitcast.18), calls=%async_computation.1 | async-start | bytes 8388608 | tf_op jit(solution)/shard_map/all_to_all | solution.py:318
  132.1 59.1 %all-to-all-start.2 = ((bf16[64,8,4096]{2,1,0:T(8,128)(2,1)}), bf16[64,8,4096]{2,1,0:T(8,128)(2,1)}, u32[]{:S(2)}, u32[]{:S(2)}) async-start(bf16[64,8,4096]{2,1,0:T(8,128)(2,1)} %bitcast.29), calls=%async_computation.2 | async-start | bytes 8388608 | tf_op jit(solution)/shard_map/all_to_all | solution.py:318
  141.0 63.1 %collective-permute-start.3 = (bf16[512,4096]{1,0:T(8,128)(2,1)}, bf16[512,4096]{1,0:T(8,128)(2,1)}, u32[]{:S(2)}, u32[]{:S(2)}) collective-permute-start(bf16[512,4096]{1,0:T(8,128)(2,1)} %bitcast.3.x_ref.x_near), channel_id=1, source_target_pairs={{0,64},{64,0},{1,65},{65,1},{2,66},{66,2},{3,67},{67,3},{4,68},{68... | collective-permute-start | bytes 12582920 | tf_op jit(solution)/shard_map/ppermute | solution.py:322
  141.1 75.5 %collective-permute-start.6 = (bf16[512,4096]{1,0:T(8,128)(2,1)}, bf16[512,4096]{1,0:T(8,128)(2,1)}, u32[]{:S(2)}, u32[]{:S(2)}) collective-permute-start(bf16[512,4096]{1,0:T(8,128)(2,1)} %bitcast.8.g_ref.g_near), channel_id=1, source_target_pairs={{0,64},{64,0},{1,65},{65,1},{2,66},{66,2},{3,67},{67,3},{4,68},{68... | collective-permute-start | bytes 12582920 | tf_op jit(solution)/shard_map/ppermute | solution.py:322
  191.2 6.1 %copy-start.7 = (bf16[512,384]{1,0:T(8,128)(2,1)S(1)}, bf16[512,384]{1,0:T(8,128)(2,1)}, u32[]{:S(2)}) copy-start(bf16[512,384]{1,0:T(8,128)(2,1)} %get-tuple-element.51) | copy-start | bytes 1179652
  191.2 6.2 %copy-start.6 = (bf16[512,384]{1,0:T(8,128)(2,1)S(1)}, bf16[512,384]{1,0:T(8,128)(2,1)}, u32[]{:S(2)}) copy-start(bf16[512,384]{1,0:T(8,128)(2,1)} %get-tuple-element.53) | copy-start | bytes 1179652
  191.2 6.7 %copy-start.5 = (bf16[512,384]{1,0:T(8,128)(2,1)S(1)}, bf16[512,384]{1,0:T(8,128)(2,1)}, u32[]{:S(2)}) copy-start(bf16[512,384]{1,0:T(8,128)(2,1)} %get-tuple-element.57) | copy-start | bytes 1179652
  191.2 55.3 %all-to-all-start.3 = ((bf16[64,8,4096]{2,1,0:T(8,128)(2,1)}), bf16[64,8,4096]{2,1,0:T(8,128)(2,1)}, u32[]{:S(2)}, u32[]{:S(2)}) async-start(bf16[64,8,4096]{2,1,0:T(8,128)(2,1)} %bitcast.28), calls=%async_computation.3 | async-start | bytes 8388608 | tf_op jit(solution)/shard_map/all_to_all | solution.py:318
  197.3 6.8 %collective-permute-start.4 = (bf16[512,384]{1,0:T(8,128)(2,1)S(1)}, bf16[512,384]{1,0:T(8,128)(2,1)S(1)}, u32[]{:S(2)}, u32[]{:S(2)}) collective-permute-start(bf16[512,384]{1,0:T(8,128)(2,1)S(1)} %copy-done.7), channel_id=1, source_target_pairs={{0,64},{64,0},{1,65},{65,1},{2,66},{66,2},{3,67},{67,3},{4,68},{68... | collective-permute-start | bytes 1179656 | tf_op jit(solution)/shard_map/ppermute | solution.py:322
  197.4 6.7 %collective-permute-start.5 = (bf16[512,384]{1,0:T(8,128)(2,1)S(1)}, bf16[512,384]{1,0:T(8,128)(2,1)S(1)}, u32[]{:S(2)}, u32[]{:S(2)}) collective-permute-start(bf16[512,384]{1,0:T(8,128)(2,1)S(1)} %copy-done.6), channel_id=1, source_target_pairs={{0,64},{64,0},{1,65},{65,1},{2,66},{66,2},{3,67},{67,3},{4,68},{68... | collective-permute-start | bytes 1179656 | tf_op jit(solution)/shard_map/ppermute | solution.py:322
  197.9 18.7 %collective-permute-start.7 = (bf16[512,384]{1,0:T(8,128)(2,1)S(1)}, bf16[512,384]{1,0:T(8,128)(2,1)S(1)}, u32[]{:S(2)}, u32[]{:S(2)}) collective-permute-start(bf16[512,384]{1,0:T(8,128)(2,1)S(1)} %copy-done.5), channel_id=1, source_target_pairs={{0,64},{64,0},{1,65},{65,1},{2,66},{66,2},{3,67},{67,3},{4,68},{68... | collective-permute-start | bytes 1179656 | tf_op jit(solution)/shard_map/ppermute | solution.py:322
  204.1 0.7 copy-start.8
  204.8 0.8 copy-start.9
  216.6 0.8 copy-start.4

commit v4 on v3

--- a/solution.py
+++ b/solution.py
@@ -35,23 +35,61 @@
     return [slots == row for row in slot_rows(routes_ref, ep_size, capacity)]
 
 
-def dispatch_tokens_kernel(ep_size, capacity, routes_ref, x_ref, out_ref):
-    masks = slot_masks(routes_ref, ep_size, capacity)
-    pick = functools.reduce(jnp.logical_or, masks).astype(jnp.bfloat16)
-    out_ref[...] = jnp.dot(pick, x_ref[...], preferred_element_type=jnp.float32).astype(
-        jnp.bfloat16
-    )
-
-
-def dispatch_grads_kernel(ep_size, capacity, routes_ref, weights_ref, x_ref, out_ref):
-    masks = slot_masks(routes_ref, ep_size, capacity)
+def place_grads(sizes, routes_ref, weights_ref, g_ref, rows, rows_hbm, sems):
+    masks = slot_masks(routes_ref, *sizes)
     pick = functools.reduce(jnp.logical_or, masks).astype(jnp.bfloat16)
     scale = sum(
         jnp.sum(jnp.where(masks[k], weights_ref[k : k + 1, :], 0.0), axis=1, keepdims=True)
         for k in range(TOP)
     )
-    rows = jnp.dot(pick, x_ref[...], preferred_element_type=jnp.float32)
-    out_ref[...] = (rows * scale).astype(jnp.bfloat16)
+    half = rows.shape[1] // 2
+    copies = []
+    for i in range(2):
+        at = pl.ds(i * half, half)
+        placed = jnp.dot(pick, g_ref[:, at], preferred_element_type=jnp.float32)
+        rows[:, at] = (placed * scale).astype(jnp.bfloat16)
+        copies.append(pltpu.make_async_copy(rows.at[:, at], rows_hbm.at[:, at], sems.at[1 + i]))
+        copies[-1].start()
+    for copy in copies:
+        copy.wait()
+
+
+def dispatch_tokens_kernel(
+    sizes, routes_ref, weights_ref, x_ref, g_hbm, out_ref, early_hbm, pick_ref, g_ref, rows, sems
+):
+    step = pl.program_id(0)
+    first = step == 0
+    early = lax.axis_index("tp") == 0
+    load = pltpu.make_async_copy(g_hbm, g_ref, sems.at[0])
+
+    @pl.when(jnp.logical_and(early, first))
+    def _():
+        load.start()
+
+    @pl.when(first)
+    def _():
+        masks = slot_masks(routes_ref, *sizes)
+        pick_ref[...] = functools.reduce(jnp.logical_or, masks).astype(jnp.bfloat16)
+
+    out_ref[...] = jnp.dot(
+        pick_ref[...], x_ref[...], preferred_element_type=jnp.float32
+    ).astype(jnp.bfloat16)
+
+    @pl.when(jnp.logical_and(early, step == pl.num_programs(0) - 1))
+    def _():
+        load.wait()
+        place_grads(sizes, routes_ref, weights_ref, g_ref, rows, early_hbm, sems)
+
+
+def dispatch_grads_kernel(
+    sizes, routes_ref, weights_ref, g_hbm, early_hbm, out_hbm, g_ref, rows, sems
+):
+    @pl.when(lax.axis_index("tp") != 0)
+    def _():
+        load = pltpu.make_async_copy(g_hbm, g_ref, sems.at[0])
+        load.start()
+        load.wait()
+        place_grads(sizes, routes_ref, weights_ref, g_ref, rows, out_hbm, sems)
 
 
 def split_weight(value):
@@ -336,15 +374,24 @@
     params = pltpu.CompilerParams(vmem_limit_bytes=56 * 1024 * 1024)
     sizes = (ep_size, capacity)
 
-    sent_tokens = pl.pallas_call(
-        functools.partial(dispatch_tokens_kernel, *sizes),
+    anywhere = pl.BlockSpec(memory_space=pl.ANY)
+    inside = pl.BlockSpec(memory_space=pltpu.VMEM)
+    sent = jax.ShapeDtypeStruct((slots, width), jnp.bfloat16)
+    place = [
+        pltpu.VMEM((token_count, width), jnp.bfloat16),
+        pltpu.VMEM((slots, width), jnp.bfloat16),
+        pltpu.SemaphoreType.DMA((3,)),
+    ]
+    sent_tokens, early_grads = pl.pallas_call(
+        functools.partial(dispatch_tokens_kernel, sizes),
         grid=grid,
-        in_specs=[small, columns(token_count, broad)],
-        out_specs=columns(slots, broad),
-        out_shape=jax.ShapeDtypeStruct((slots, width), jnp.bfloat16),
+        in_specs=[small, small, columns(token_count, broad), anywhere],
+        out_specs=[columns(slots, broad), anywhere],
+        out_shape=[sent, sent],
+        scratch_shapes=[pltpu.VMEM((slots, token_count), jnp.bfloat16)] + place,
         compiler_params=params,
         name="dispatch_tokens",
-    )(routes_t, tokens)
+    )(routes_t, weights_t, tokens, upstream)
     gate_mat, up_mat, down_mat = gate_weight[0], up_weight[0], down_weight[0]
     gate = (gate_mat, swap(gate_mat))
     up = (up_mat, swap(up_mat))
@@ -354,15 +401,15 @@
     )
     gate, up, down = (gate_mat, gate_b), (up_mat, up_b), (down_mat, down_b)
     sent_grads = pl.pallas_call(
-        functools.partial(dispatch_grads_kernel, *sizes),
-        grid=grid,
-        in_specs=[small, small, columns(token_count, broad)],
-        out_specs=columns(slots, broad),
-        out_shape=jax.ShapeDtypeStruct((slots, width), jnp.bfloat16),
+        functools.partial(dispatch_grads_kernel, sizes),
+        in_specs=[inside, inside, anywhere, anywhere],
+        out_specs=anywhere,
+        out_shape=sent,
+        input_output_aliases={3: 0},
+        scratch_shapes=place,
         compiler_params=params,
         name="dispatch_grads",
-    )(routes_t, weights_late, upstream)
-
+    )(routes_t, weights_late, upstream, early_grads)
     forward, backward = expert_calls(slots, width, gate_mat.shape[1], block, params)
 
     inputs = to_experts(sent_tokens, ep_size)

time: 251 us -> 249 us (level)
  transfers between devices with their start and end apart: 12 -> 12, of which waited for: 6 -> 6; matrix products, arithmetic and copies ran while one was open for 0% -> 0% of each run, Pallas kernels for 27% -> 26%
where the time goes in v4:
time: 249 us; the launch traced here: 248 us
  waiting for transfers between devices  128 us (51%)
  Pallas kernels  74.6 us (30%)
  starting transfers between devices  38 us (15%)
  local copies, waits for them, and re-layouts  7.3 us (3%)
    all_to_all x4, waiting for transfers between devices, to_experts(): lax.all_to_all(blocks, 'ep', split_axis=0, concat_axis=0, tiled=True)  117 us
    all_to_all x4, starting transfers between devices, to_experts(): lax.all_to_all(blocks, 'ep', split_axis=0, concat_axis=0, tiled=True)  36 us
    pallas_call x1, Pallas kernels, on_device(): backward(grads, pre, *down, *gate, *up)  19.5 us
    pallas_call x1, Pallas kernels, on_device(): out, pre, hidden_a, hidden_b = forward(inputs, *gate, *up, *down)  19 us
    ppermute x8, waiting for transfers between devices, swap(): return lax.ppermute(rows, 'tp', SWAP)  10.9 us
    pallas_call x1, Pallas kernels, grads_of_gate_up(): pl.pallas_call(gate_up_kernel, grid=(width // block,), in_specs=[rows, ro...  10.9 us
    pallas_call x1, Pallas kernels, grads_of_down(): pl.pallas_call(down_kernel, grid=(width // block,), in_specs=[rows, rows,...  7.68 us
    unnamed x20, local copies, waits for them, and re-layouts  7.3 us
  transfers between devices with their start and end apart: 12, of which 6 were waited for; matrix products, arithmetic and copies ran while one was open for 0% of the time, Pallas kernels for 26%

profile of v4, /device:TPU:2, one launch (start us, length us, event | category | flops | bytes accessed | tf_op | source)
XLA Modules:
  0.0 248.5 jit_solution(5202309489299577468)
XLA Ops:
  0.6 7.1 %dispatch_tokens.1 = (bf16[512,4096]{1,0:T(8,128)(2,1)}, bf16[512,4096]{1,0:T(8,128)(2,1)}) custom-call(s32[2,128]{1,0:T(2,128)} %bitcast.31, f32[2,128]{1,0:T(2,128)} %bitcast.35, bf16[128,4096]{1,0:T(8,128)(2,1)} %x_ref.1, bf16[128,4096]{1,0:T(8,128)(2,1)} %upstream_ref.1), custom_call_target="tpu_custom_call" | custom-call | tf_op jit(solution)/shard_map/dispatch_tokens/pallas_call | solution.py:385
  7.7 0.0 copy-start
  7.7 12.0 %all-to-all-start = ((bf16[64,8,4096]{2,1,0:T(8,128)(2,1)}), bf16[64,8,4096]{2,1,0:T(8,128)(2,1)}, u32[]{:S(2)}, u32[]{:S(2)}) async-start(bf16[64,8,4096]{2,1,0:T(8,128)(2,1)} %bitcast.29), calls=%async_computation | async-start | bytes 8388608 | tf_op jit(solution)/shard_map/all_to_all | solution.py:356
  19.7 0.0 copy-done
  19.7 0.1 collective-permute-start
  19.8 0.5 collective-permute-start.1
  20.3 0.1 collective-permute-start.2
  20.4 8.6 %collective-permute-done.gate_b = bf16[4096,384]{1,0:T(8,128)(2,1)S(1)} collective-permute-done((bf16[4096,384]{1,0:T(8,128)(2,1)S(1)}, bf16[4096,384]{1,0:T(8,128)(2,1)S(1)}, u32[]{:S(2)}, u32[]{:S(2)}) %collective-permute-start) | collective-permute-done | bytes 3145760 | tf_op jit(solution)/shard_map/ppermute | solution.py:360
  29.0 0.0 copy-start.1
  29.0 1.7 copy-done.1
  30.7 0.0 collective-permute-done.1.up_b
  30.7 0.0 copy-start.2
  30.7 1.7 copy-done.2
  32.4 2.3 collective-permute-done.2.down_b
  34.7 0.0 copy-start.3
  34.7 1.7 copy-done.3
  36.3 0.7 dispatch_grads.1
  37.1 31.4 %all-to-all-done = bf16[64,8,4096]{2,1,0:T(8,128)(2,1)} async-done(((bf16[64,8,4096]{2,1,0:T(8,128)(2,1)}), bf16[64,8,4096]{2,1,0:T(8,128)(2,1)}, u32[]{:S(2)}, u32[]{:S(2)}) %all-to-all-start) | async-done | bytes 4194336 | tf_op jit(solution)/shard_map/all_to_all | solution.py:356
  68.4 7.6 %all-to-all-start.1 = ((bf16[64,8,4096]{2,1,0:T(8,128)(2,1)}), bf16[64,8,4096]{2,1,0:T(8,128)(2,1)}, u32[]{:S(2)}, u32[]{:S(2)}) async-start(bf16[64,8,4096]{2,1,0:T(8,128)(2,1)} %bitcast.17), calls=%async_computation.1 | async-start | bytes 8388608 | tf_op jit(solution)/shard_map/all_to_all | solution.py:356
  76.0 19.0 %forward.1 = (bf16[512,4096]{1,0:T(8,128)(2,1)}, f32[512,1536]{1,0:T(8,128)}, bf16[512,384]{1,0:T(8,128)(2,1)}, bf16[512,384]{1,0:T(8,128)(2,1)}) custom-call(bf16[512,4096]{1,0:T(8,128)(2,1)} %bitcast.3.x_ref.x_near, bf16[4096,384]{1,0:T(8,128)(2,1)} %bitcast.18, bf16[4096,384]{1,0:T(8,128)(2,1)} %copy-done.1, bf16[4096,384]{1,0:T(8,128)(2,1)} %bitcast.22, ...), custom_call_target="tpu_custom_call" | custom-call | flops 1 | bytes 1 | tf_op jit(solution)/shard_map/forward/pallas_call | solution.py:418
  95.0 31.8 %all-to-all-done.1 = bf16[64,8,4096]{2,1,0:T(8,128)(2,1)} async-done(((bf16[64,8,4096]{2,1,0:T(8,128)(2,1)}), bf16[64,8,4096]{2,1,0:T(8,128)(2,1)}, u32[]{:S(2)}, u32[]{:S(2)}) %all-to-all-start.1) | async-done | bytes 4194336 | tf_op jit(solution)/shard_map/all_to_all | solution.py:356
  126.8 9.6 %all-to-all-start.2 = ((bf16[64,8,4096]{2,1,0:T(8,128)(2,1)}), bf16[64,8,4096]{2,1,0:T(8,128)(2,1)}, u32[]{:S(2)}, u32[]{:S(2)}) async-start(bf16[64,8,4096]{2,1,0:T(8,128)(2,1)} %bitcast.28), calls=%async_computation.2 | async-start | bytes 8388608 | tf_op jit(solution)/shard_map/all_to_all | solution.py:356
  136.4 0.1 collective-permute-start.3
  136.5 0.5 collective-permute-start.6
  137.0 19.5 %backward.1 = (bf16[512,4096]{1,0:T(8,128)(2,1)}, bf16[512,384]{1,0:T(8,128)(2,1)}, bf16[512,384]{1,0:T(8,128)(2,1)}, bf16[512,384]{1,0:T(8,128)(2,1)}, bf16[512,384]{1,0:T(8,128)(2,1)}) custom-call(bf16[512,4096]{1,0:T(8,128)(2,1)} %bitcast.8.g_ref.g_near, f32[512,1536]{1,0:T(8,128)} %get-tuple-element.45.pre, bf16[384,4096]{1,0:T(8,128)(2,1)} %bitcast.26, ...), custom_call_target="tpu_custom_call" | custom-call | flops 1 | bytes 1 | tf_op jit(solution)/shard_map/backward/pallas_call | solution.py:421
  156.5 29.1 %all-to-all-done.2 = bf16[64,8,4096]{2,1,0:T(8,128)(2,1)} async-done(((bf16[64,8,4096]{2,1,0:T(8,128)(2,1)}), bf16[64,8,4096]{2,1,0:T(8,128)(2,1)}, u32[]{:S(2)}, u32[]{:S(2)}) %all-to-all-start.2) | async-done | bytes 4194336 | tf_op jit(solution)/shard_map/all_to_all | solution.py:356
  185.6 0.0 copy-start.7
  185.6 0.0 copy-start.6
  185.6 0.0 copy-start.5
  185.6 6.9 %all-to-all-start.3 = ((bf16[64,8,4096]{2,1,0:T(8,128)(2,1)}), bf16[64,8,4096]{2,1,0:T(8,128)(2,1)}, u32[]{:S(2)}, u32[]{:S(2)}) async-start(bf16[64,8,4096]{2,1,0:T(8,128)(2,1)} %bitcast.27), calls=%async_computation.3 | async-start | bytes 8388608 | tf_op jit(solution)/shard_map/all_to_all | solution.py:356
  192.5 0.0 copy-done.7
  192.5 0.1 collective-permute-start.4
  192.6 0.0 copy-done.6
  192.6 0.5 collective-permute-start.5
  193.1 0.0 copy-done.5
  193.1 0.1 collective-permute-start.7
  193.2 6.0 %combine_outputs.1 = (bf16[128,4096]{1,0:T(8,128)(2,1)}, f32[2,128]{1,0:T(2,128)}) custom-call(s32[2,128]{1,0:T(2,128)} %bitcast.33, f32[2,128]{1,0:T(2,128)} %bitcast.37, bf16[128,4096]{1,0:T(8,128)(2,1)} %upstream_ref.1, bf16[512,4096]{1,0:T(8,128)(2,1)} %bitcast.10.rows_ref), custom_call_target="tpu_custom_call" | custom-call | flops 1610612736 | bytes 5242880 | tf_op jit(solution)/shard_map/combine_outputs/pallas_call | solution.py:431
  199.3 0.0 collective-permute-done.3.x_far
  199.3 0.0 collective-permute-done.4.d_gate_far
  199.3 0.0 copy-start.8
  199.3 0.0 collective-permute-done.5.d_up_far
  199.3 0.7 copy-done.8
  200.0 0.0 copy-start.9
  200.0 0.8 copy-done.9
  200.8 10.9 %grad_gate_up.1 = (bf16[4096,384]{1,0:T(8,128)(2,1)}, bf16[4096,384]{1,0:T(8,128)(2,1)}) custom-call(bf16[512,4096]{1,0:T(8,128)(2,1)} %bitcast.3.x_ref.x_near, bf16[512,4096]{1,0:T(8,128)(2,1)} %collective-permute-done.3.x_far, bf16[512,384]{1,0:T(8,128)(2,1)} %get-tuple-element.54.d_gate_near, bf16[512,384]{1,0:T(8,128)(2,1)} %copy-done.8, ...), custom_call_target="tpu_custom_call" | custom-call | flops 6442450944 | bytes 8388608 | tf_op jit(solution)/shard_map/grad_gate_up/pallas_call | solution.py:317
  211.7 0.0 collective-permute-done.7.hidden_far
  211.7 0.0 copy-start.4
  211.7 0.0 collective-permute-done.6.g_far
  211.7 0.8 copy-done.4
  212.5 7.7 %grad_down.1 = bf16[384,4096]{1,0:T(8,128)(2,1)} custom-call(bf16[512,4096]{1,0:T(8,128)(2,1)} %bitcast.8.g_ref.g_near, bf16[512,4096]{1,0:T(8,128)(2,1)} %collective-permute-done.6.g_far, bf16[512,384]{1,0:T(8,128)(2,1)} %get-tuple-element.60.hidden_near, bf16[512,384]{1,0:T(8,128)(2,1)} %copy-done.4), custom_call_target="tpu_custom_call" | custom-call | flops 3221225472 | bytes 8388608 | tf_op jit(solution)/shard_map/grad_down/pallas_call | solution.py:334
  220.1 24.6 %all-to-all-done.3 = bf16[64,8,4096]{2,1,0:T(8,128)(2,1)} async-done(((bf16[64,8,4096]{2,1,0:T(8,128)(2,1)}), bf16[64,8,4096]{2,1,0:T(8,128)(2,1)}, u32[]{:S(2)}, u32[]{:S(2)}) %all-to-all-start.3) | async-done | bytes 4194336 | tf_op jit(solution)/shard_map/all_to_all | solution.py:356
  244.8 3.7 %combine_grads.1 = bf16[128,4096]{1,0:T(8,128)(2,1)} custom-call(s32[2,128]{1,0:T(2,128)} %bitcast.34, bf16[512,4096]{1,0:T(8,128)(2,1)} %bitcast.12.rows_ref), custom_call_target="tpu_custom_call" | custom-call | tf_op jit(solution)/shard_map/combine_grads/pallas_call | solution.py:445
Async XLA Ops:
  7.7 12.0 %copy-start = (bf16[1,4096,384]{2,1,0:T(8,128)(2,1)S(1)}, bf16[1,4096,384]{2,1,0:T(8,128)(2,1)}, u32[]{:S(2)}) copy-start(bf16[1,4096,384]{2,1,0:T(8,128)(2,1)} %param.11) | copy-start | bytes 9437188
  7.7 60.7 %all-to-all-start = ((bf16[64,8,4096]{2,1,0:T(8,128)(2,1)}), bf16[64,8,4096]{2,1,0:T(8,128)(2,1)}, u32[]{:S(2)}, u32[]{:S(2)}) async-start(bf16[64,8,4096]{2,1,0:T(8,128)(2,1)} %bitcast.29), calls=%async_computation | async-start | bytes 8388608 | tf_op jit(solution)/shard_map/all_to_all | solution.py:356
  19.7 9.3 %collective-permute-start = (bf16[4096,384]{1,0:T(8,128)(2,1)S(1)}, bf16[4096,384]{1,0:T(8,128)(2,1)S(1)}, u32[]{:S(2)}, u32[]{:S(2)}) collective-permute-start(bf16[4096,384]{1,0:T(8,128)(2,1)S(1)} %bitcast.20), channel_id=1, source_target_pairs={{0,64},{64,0},{1,65},{65,1},{2,66},{66,2},{3,67},{67,3},{4,68},{68... | collective-permute-start | bytes 9437192 | tf_op jit(solution)/shard_map/ppermute | solution.py:360
  19.8 10.9 %collective-permute-start.1 = (bf16[4096,384]{1,0:T(8,128)(2,1)}, bf16[4096,384]{1,0:T(8,128)(2,1)S(1)}, u32[]{:S(2)}, u32[]{:S(2)}) collective-permute-start(bf16[4096,384]{1,0:T(8,128)(2,1)} %bitcast.21), channel_id=1, source_target_pairs={{0,64},{64,0},{1,65},{65,1},{2,66},{66,2},{3,67},{67,3},{4,68},{68... | collective-permute-start | bytes 9437192 | tf_op jit(solution)/shard_map/ppermute | solution.py:360
  20.3 14.4 %collective-permute-start.2 = (bf16[384,4096]{1,0:T(8,128)(2,1)}, bf16[384,4096]{1,0:T(8,128)(2,1)S(1)}, u32[]{:S(2)}, u32[]{:S(2)}) collective-permute-start(bf16[384,4096]{1,0:T(8,128)(2,1)} %bitcast.24), channel_id=1, source_target_pairs={{0,64},{64,0},{1,65},{65,1},{2,66},{66,2},{3,67},{67,3},{4,68},{68... | collective-permute-start | bytes 9437192 | tf_op jit(solution)/shard_map/ppermute | solution.py:360
  29.0 1.7 copy-start.1
  30.7 1.7 copy-start.2
  34.7 1.7 copy-start.3
  68.4 58.4 %all-to-all-start.1 = ((bf16[64,8,4096]{2,1,0:T(8,128)(2,1)}), bf16[64,8,4096]{2,1,0:T(8,128)(2,1)}, u32[]{:S(2)}, u32[]{:S(2)}) async-start(bf16[64,8,4096]{2,1,0:T(8,128)(2,1)} %bitcast.17), calls=%async_computation.1 | async-start | bytes 8388608 | tf_op jit(solution)/shard_map/all_to_all | solution.py:356
  126.8 58.8 %all-to-all-start.2 = ((bf16[64,8,4096]{2,1,0:T(8,128)(2,1)}), bf16[64,8,4096]{2,1,0:T(8,128)(2,1)}, u32[]{:S(2)}, u32[]{:S(2)}) async-start(bf16[64,8,4096]{2,1,0:T(8,128)(2,1)} %bitcast.28), calls=%async_computation.2 | async-start | bytes 8388608 | tf_op jit(solution)/shard_map/all_to_all | solution.py:356
  136.4 62.9 %collective-permute-start.3 = (bf16[512,4096]{1,0:T(8,128)(2,1)}, bf16[512,4096]{1,0:T(8,128)(2,1)}, u32[]{:S(2)}, u32[]{:S(2)}) collective-permute-start(bf16[512,4096]{1,0:T(8,128)(2,1)} %bitcast.3.x_ref.x_near), channel_id=1, source_target_pairs={{0,64},{64,0},{1,65},{65,1},{2,66},{66,2},{3,67},{67,3},{4,68},{68... | collective-permute-start | bytes 12582920 | tf_op jit(solution)/shard_map/ppermute | solution.py:360
  136.5 75.2 %collective-permute-start.6 = (bf16[512,4096]{1,0:T(8,128)(2,1)}, bf16[512,4096]{1,0:T(8,128)(2,1)}, u32[]{:S(2)}, u32[]{:S(2)}) collective-permute-start(bf16[512,4096]{1,0:T(8,128)(2,1)} %bitcast.8.g_ref.g_near), channel_id=1, source_target_pairs={{0,64},{64,0},{1,65},{65,1},{2,66},{66,2},{3,67},{67,3},{4,68},{68... | collective-permute-start | bytes 12582920 | tf_op jit(solution)/shard_map/ppermute | solution.py:360
  185.6 6.9 %copy-start.7 = (bf16[512,384]{1,0:T(8,128)(2,1)S(1)}, bf16[512,384]{1,0:T(8,128)(2,1)}, u32[]{:S(2)}) copy-start(bf16[512,384]{1,0:T(8,128)(2,1)} %get-tuple-element.55) | copy-start | bytes 1179652
  185.6 7.0 %copy-start.6 = (bf16[512,384]{1,0:T(8,128)(2,1)S(1)}, bf16[512,384]{1,0:T(8,128)(2,1)}, u32[]{:S(2)}) copy-start(bf16[512,384]{1,0:T(8,128)(2,1)} %get-tuple-element.57) | copy-start | bytes 1179652
  185.6 7.5 %copy-start.5 = (bf16[512,384]{1,0:T(8,128)(2,1)S(1)}, bf16[512,384]{1,0:T(8,128)(2,1)}, u32[]{:S(2)}) copy-start(bf16[512,384]{1,0:T(8,128)(2,1)} %get-tuple-element.61) | copy-start | bytes 1179652
  185.6 59.2 %all-to-all-start.3 = ((bf16[64,8,4096]{2,1,0:T(8,128)(2,1)}), bf16[64,8,4096]{2,1,0:T(8,128)(2,1)}, u32[]{:S(2)}, u32[]{:S(2)}) async-start(bf16[64,8,4096]{2,1,0:T(8,128)(2,1)} %bitcast.27), calls=%async_computation.3 | async-start | bytes 8388608 | tf_op jit(solution)/shard_map/all_to_all | solution.py:356
  192.5 6.7 %collective-permute-start.4 = (bf16[512,384]{1,0:T(8,128)(2,1)S(1)}, bf16[512,384]{1,0:T(8,128)(2,1)S(1)}, u32[]{:S(2)}, u32[]{:S(2)}) collective-permute-start(bf16[512,384]{1,0:T(8,128)(2,1)S(1)} %copy-done.7), channel_id=1, source_target_pairs={{0,64},{64,0},{1,65},{65,1},{2,66},{66,2},{3,67},{67,3},{4,68},{68... | collective-permute-start | bytes 1179656 | tf_op jit(solution)/shard_map/ppermute | solution.py:360
  192.6 6.7 %collective-permute-start.5 = (bf16[512,384]{1,0:T(8,128)(2,1)S(1)}, bf16[512,384]{1,0:T(8,128)(2,1)S(1)}, u32[]{:S(2)}, u32[]{:S(2)}) collective-permute-start(bf16[512,384]{1,0:T(8,128)(2,1)S(1)} %copy-done.6), channel_id=1, source_target_pairs={{0,64},{64,0},{1,65},{65,1},{2,66},{66,2},{3,67},{67,3},{4,68},{68... | collective-permute-start | bytes 1179656 | tf_op jit(solution)/shard_map/ppermute | solution.py:360
  193.1 18.6 %collective-permute-start.7 = (bf16[512,384]{1,0:T(8,128)(2,1)S(1)}, bf16[512,384]{1,0:T(8,128)(2,1)S(1)}, u32[]{:S(2)}, u32[]{:S(2)}) collective-permute-start(bf16[512,384]{1,0:T(8,128)(2,1)S(1)} %copy-done.5), channel_id=1, source_target_pairs={{0,64},{64,0},{1,65},{65,1},{2,66},{66,2},{3,67},{67,3},{4,68},{68... | collective-permute-start | bytes 1179656 | tf_op jit(solution)/shard_map/ppermute | solution.py:360
  199.3 0.7 copy-start.8
  200.0 0.8 copy-start.9
  211.7 0.8 copy-start.4

commit v5 on v4

--- a/solution.py
+++ b/solution.py
@@ -105,7 +105,7 @@
 
 
 def combine_outputs_kernel(
-    ep_size, capacity, routes_ref, weights_ref, upstream_ref, rows_ref, mixed_ref, route_ref, acc
+    ep_size, capacity, routes_ref, weights_ref, upstream_ref, rows_ref, mixed_ref, route_ref, pick_ref, acc
 ):
     step = pl.program_id(0)
     masks = slot_masks(routes_ref, ep_size, capacity)
@@ -119,6 +119,8 @@
     @pl.when(step == 0)
     def _():
         acc[...] = jnp.zeros_like(acc)
+        pick = functools.reduce(jnp.logical_or, masks).astype(jnp.float32)
+        pick_ref[...] = pick.T.astype(jnp.bfloat16)
 
     acc[...] += lax.dot_general(
         rows, upstream_ref[...], (((1,), (1,)), ((), ())), preferred_element_type=jnp.float32
@@ -132,10 +134,10 @@
             )
 
 
-def combine_grads_kernel(ep_size, capacity, routes_ref, rows_ref, out_ref):
-    masks = slot_masks(routes_ref, ep_size, capacity)
-    pick = functools.reduce(jnp.logical_or, masks).astype(jnp.bfloat16)
-    out_ref[...] = collect_dot(pick, rows_ref[...]).astype(jnp.bfloat16)
+def combine_grads_kernel(pick_ref, rows_ref, out_ref):
+    out_ref[...] = jnp.dot(
+        pick_ref[...], rows_ref[...], preferred_element_type=jnp.float32
+    ).astype(jnp.bfloat16)
 
 
 def rows_dot(a, b):
@@ -428,14 +430,15 @@
         inputs, swap(inputs), (d_gate_a, swap(d_gate_b)), (d_up_a, swap(d_up_b)), block, params
     )
     grad_down = grads_of_down(grads, swap(grads), (hidden_a, swap(hidden_b)), block, params)
-    mixed, grad_route = pl.pallas_call(
+    mixed, grad_route, picked = pl.pallas_call(
         functools.partial(combine_outputs_kernel, *sizes),
         grid=grid,
         in_specs=[small, small, columns(token_count, broad), columns(slots, broad)],
-        out_specs=[columns(token_count, broad), small],
+        out_specs=[columns(token_count, broad), small, whole((token_count, slots))],
         out_shape=[
             jax.ShapeDtypeStruct((token_count, width), jnp.bfloat16),
             jax.ShapeDtypeStruct((TOP, token_count), jnp.float32),
+            jax.ShapeDtypeStruct((token_count, slots), jnp.bfloat16),
         ],
         scratch_shapes=[pltpu.VMEM((slots, token_count), jnp.float32)],
         compiler_params=params,
@@ -443,14 +446,14 @@
         name="combine_outputs",
     )(routes_t, weights_t, upstream, out_home)
     grad_tokens = pl.pallas_call(
-        functools.partial(combine_grads_kernel, *sizes),
+        combine_grads_kernel,
         grid=grid,
-        in_specs=[small, columns(slots, broad)],
+        in_specs=[whole((token_count, slots)), columns(slots, broad)],
         out_specs=columns(token_count, broad),
         out_shape=jax.ShapeDtypeStruct((token_count, width), jnp.bfloat16),
         compiler_params=params,
         name="combine_grads",
-    )(routes_t, back_home)
+    )(picked, back_home)
     return (mixed, grad_tokens, grad_route.T, grad_gate[None], grad_up[None], grad_down[None])
 
 

time: 249 us -> 249 us (level)
  no operation moved by 1% of the time
where the time goes in v5:
time: 249 us; the launch traced here: 248 us
  waiting for transfers between devices  128 us (51%)
  Pallas kernels  74.6 us (30%)
  starting transfers between devices  38 us (15%)
  local copies, waits for them, and re-layouts  7.3 us (3%)
    all_to_all x4, waiting for transfers between devices, to_experts(): lax.all_to_all(blocks, 'ep', split_axis=0, concat_axis=0, tiled=True)  117 us
    all_to_all x4, starting transfers between devices, to_experts(): lax.all_to_all(blocks, 'ep', split_axis=0, concat_axis=0, tiled=True)  36 us
    pallas_call x1, Pallas kernels, on_device(): backward(grads, pre, *down, *gate, *up)  19.5 us
    pallas_call x1, Pallas kernels, on_device(): out, pre, hidden_a, hidden_b = forward(inputs, *gate, *up, *down)  19 us
    ppermute x8, waiting for transfers between devices, swap(): return lax.ppermute(rows, 'tp', SWAP)  10.9 us
    pallas_call x1, Pallas kernels, grads_of_gate_up(): pl.pallas_call(gate_up_kernel, grid=(width // block,), in_specs=[rows, ro...  10.9 us
    pallas_call x1, Pallas kernels, grads_of_down(): pl.pallas_call(down_kernel, grid=(width // block,), in_specs=[rows, rows,...  7.68 us
    unnamed x20, local copies, waits for them, and re-layouts  7.3 us
  transfers between devices with their start and end apart: 12, of which 6 were waited for; matrix products, arithmetic and copies ran while one was open for 0% of the time, Pallas kernels for 26%

profile of v5, /device:TPU:2, one launch (start us, length us, event | category | flops | bytes accessed | tf_op | source)
XLA Modules:
  0.0 248.3 jit_solution(12071484674103525602)
XLA Ops:
  0.6 7.1 %dispatch_tokens.1 = (bf16[512,4096]{1,0:T(8,128)(2,1)}, bf16[512,4096]{1,0:T(8,128)(2,1)}) custom-call(s32[2,128]{1,0:T(2,128)} %bitcast.31, f32[2,128]{1,0:T(2,128)} %bitcast.34, bf16[128,4096]{1,0:T(8,128)(2,1)} %x_ref.1, bf16[128,4096]{1,0:T(8,128)(2,1)} %upstream_ref.1), custom_call_target="tpu_custom_call" | custom-call | tf_op jit(solution)/shard_map/dispatch_tokens/pallas_call | solution.py:387
  7.7 0.0 copy-start
  7.7 12.0 %all-to-all-start = ((bf16[64,8,4096]{2,1,0:T(8,128)(2,1)}), bf16[64,8,4096]{2,1,0:T(8,128)(2,1)}, u32[]{:S(2)}, u32[]{:S(2)}) async-start(bf16[64,8,4096]{2,1,0:T(8,128)(2,1)} %bitcast.29), calls=%async_computation | async-start | bytes 8388608 | tf_op jit(solution)/shard_map/all_to_all | solution.py:358
  19.7 0.0 copy-done
  19.7 0.1 collective-permute-start
  19.8 0.5 collective-permute-start.1
  20.3 0.1 collective-permute-start.2
  20.4 8.6 %collective-permute-done.gate_b = bf16[4096,384]{1,0:T(8,128)(2,1)S(1)} collective-permute-done((bf16[4096,384]{1,0:T(8,128)(2,1)S(1)}, bf16[4096,384]{1,0:T(8,128)(2,1)S(1)}, u32[]{:S(2)}, u32[]{:S(2)}) %collective-permute-start) | collective-permute-done | bytes 3145760 | tf_op jit(solution)/shard_map/ppermute | solution.py:362
  29.0 0.0 copy-start.1
  29.0 1.7 copy-done.1
  30.7 0.0 collective-permute-done.1.up_b
  30.7 0.0 copy-start.2
  30.7 1.7 copy-done.2
  32.4 2.3 collective-permute-done.2.down_b
  34.7 0.0 copy-start.3
  34.7 1.7 copy-done.3
  36.3 0.7 dispatch_grads.1
  37.1 31.4 %all-to-all-done = bf16[64,8,4096]{2,1,0:T(8,128)(2,1)} async-done(((bf16[64,8,4096]{2,1,0:T(8,128)(2,1)}), bf16[64,8,4096]{2,1,0:T(8,128)(2,1)}, u32[]{:S(2)}, u32[]{:S(2)}) %all-to-all-start) | async-done | bytes 4194336 | tf_op jit(solution)/shard_map/all_to_all | solution.py:358
  68.4 7.6 %all-to-all-start.1 = ((bf16[64,8,4096]{2,1,0:T(8,128)(2,1)}), bf16[64,8,4096]{2,1,0:T(8,128)(2,1)}, u32[]{:S(2)}, u32[]{:S(2)}) async-start(bf16[64,8,4096]{2,1,0:T(8,128)(2,1)} %bitcast.17), calls=%async_computation.1 | async-start | bytes 8388608 | tf_op jit(solution)/shard_map/all_to_all | solution.py:358
  76.0 19.0 %forward.1 = (bf16[512,4096]{1,0:T(8,128)(2,1)}, f32[512,1536]{1,0:T(8,128)}, bf16[512,384]{1,0:T(8,128)(2,1)}, bf16[512,384]{1,0:T(8,128)(2,1)}) custom-call(bf16[512,4096]{1,0:T(8,128)(2,1)} %bitcast.3.x_ref.x_near, bf16[4096,384]{1,0:T(8,128)(2,1)} %bitcast.18, bf16[4096,384]{1,0:T(8,128)(2,1)} %copy-done.1, bf16[4096,384]{1,0:T(8,128)(2,1)} %bitcast.22, ...), custom_call_target="tpu_custom_call" | custom-call | flops 1 | bytes 1 | tf_op jit(solution)/shard_map/forward/pallas_call | solution.py:420
  95.0 31.8 %all-to-all-done.1 = bf16[64,8,4096]{2,1,0:T(8,128)(2,1)} async-done(((bf16[64,8,4096]{2,1,0:T(8,128)(2,1)}), bf16[64,8,4096]{2,1,0:T(8,128)(2,1)}, u32[]{:S(2)}, u32[]{:S(2)}) %all-to-all-start.1) | async-done | bytes 4194336 | tf_op jit(solution)/shard_map/all_to_all | solution.py:358
  126.8 9.6 %all-to-all-start.2 = ((bf16[64,8,4096]{2,1,0:T(8,128)(2,1)}), bf16[64,8,4096]{2,1,0:T(8,128)(2,1)}, u32[]{:S(2)}, u32[]{:S(2)}) async-start(bf16[64,8,4096]{2,1,0:T(8,128)(2,1)} %bitcast.28), calls=%async_computation.2 | async-start | bytes 8388608 | tf_op jit(solution)/shard_map/all_to_all | solution.py:358
  136.4 0.1 collective-permute-start.3
  136.5 0.5 collective-permute-start.6
  137.0 19.5 %backward.1 = (bf16[512,4096]{1,0:T(8,128)(2,1)}, bf16[512,384]{1,0:T(8,128)(2,1)}, bf16[512,384]{1,0:T(8,128)(2,1)}, bf16[512,384]{1,0:T(8,128)(2,1)}, bf16[512,384]{1,0:T(8,128)(2,1)}) custom-call(bf16[512,4096]{1,0:T(8,128)(2,1)} %bitcast.8.g_ref.g_near, f32[512,1536]{1,0:T(8,128)} %get-tuple-element.46.pre, bf16[384,4096]{1,0:T(8,128)(2,1)} %bitcast.26, ...), custom_call_target="tpu_custom_call" | custom-call | flops 1 | bytes 1 | tf_op jit(solution)/shard_map/backward/pallas_call | solution.py:423
  156.5 29.1 %all-to-all-done.2 = bf16[64,8,4096]{2,1,0:T(8,128)(2,1)} async-done(((bf16[64,8,4096]{2,1,0:T(8,128)(2,1)}), bf16[64,8,4096]{2,1,0:T(8,128)(2,1)}, u32[]{:S(2)}, u32[]{:S(2)}) %all-to-all-start.2) | async-done | bytes 4194336 | tf_op jit(solution)/shard_map/all_to_all | solution.py:358
  185.6 0.0 copy-start.7
  185.6 0.0 copy-start.6
  185.6 0.0 copy-start.5
  185.6 6.9 %all-to-all-start.3 = ((bf16[64,8,4096]{2,1,0:T(8,128)(2,1)}), bf16[64,8,4096]{2,1,0:T(8,128)(2,1)}, u32[]{:S(2)}, u32[]{:S(2)}) async-start(bf16[64,8,4096]{2,1,0:T(8,128)(2,1)} %bitcast.27), calls=%async_computation.3 | async-start | bytes 8388608 | tf_op jit(solution)/shard_map/all_to_all | solution.py:358
  192.5 0.0 copy-done.7
  192.5 0.1 collective-permute-start.4
  192.6 0.0 copy-done.6
  192.6 0.5 collective-permute-start.5
  193.1 0.0 copy-done.5
  193.1 0.1 collective-permute-start.7
  193.2 6.2 %combine_outputs.1 = (bf16[128,4096]{1,0:T(8,128)(2,1)}, f32[2,128]{1,0:T(2,128)}, bf16[128,512]{1,0:T(8,128)(2,1)}) custom-call(s32[2,128]{1,0:T(2,128)} %bitcast.33, f32[2,128]{1,0:T(2,128)} %bitcast.36, bf16[128,4096]{1,0:T(8,128)(2,1)} %upstream_ref.1, bf16[512,4096]{1,0:T(8,128)(2,1)} %bitcast.10.rows_ref), custom_call_target="tpu_custom_call" | custom-call | flops 1610612736 | bytes 5242880 | tf_op jit(solution)/shard_map/combine_outputs/pallas_call | solution.py:433
  199.4 0.0 collective-permute-done.3.x_far
  199.4 0.0 collective-permute-done.4.d_gate_far
  199.4 0.0 copy-start.8
  199.5 0.0 collective-permute-done.5.d_up_far
  199.5 0.7 copy-done.8
  200.2 0.0 copy-start.9
  200.2 0.8 copy-done.9
  201.0 10.9 %grad_gate_up.1 = (bf16[4096,384]{1,0:T(8,128)(2,1)}, bf16[4096,384]{1,0:T(8,128)(2,1)}) custom-call(bf16[512,4096]{1,0:T(8,128)(2,1)} %bitcast.3.x_ref.x_near, bf16[512,4096]{1,0:T(8,128)(2,1)} %collective-permute-done.3.x_far, bf16[512,384]{1,0:T(8,128)(2,1)} %get-tuple-element.56.d_gate_near, bf16[512,384]{1,0:T(8,128)(2,1)} %copy-done.8, ...), custom_call_target="tpu_custom_call" | custom-call | flops 6442450944 | bytes 8388608 | tf_op jit(solution)/shard_map/grad_gate_up/pallas_call | solution.py:319
  211.9 0.0 collective-permute-done.7.hidden_far
  211.9 0.0 copy-start.4
  211.9 0.0 collective-permute-done.6.g_far
  211.9 0.8 copy-done.4
  212.6 7.7 %grad_down.1 = bf16[384,4096]{1,0:T(8,128)(2,1)} custom-call(bf16[512,4096]{1,0:T(8,128)(2,1)} %bitcast.8.g_ref.g_near, bf16[512,4096]{1,0:T(8,128)(2,1)} %collective-permute-done.6.g_far, bf16[512,384]{1,0:T(8,128)(2,1)} %get-tuple-element.62.hidden_near, bf16[512,384]{1,0:T(8,128)(2,1)} %copy-done.4), custom_call_target="tpu_custom_call" | custom-call | flops 3221225472 | bytes 8388608 | tf_op jit(solution)/shard_map/grad_down/pallas_call | solution.py:336
  220.3 24.5 %all-to-all-done.3 = bf16[64,8,4096]{2,1,0:T(8,128)(2,1)} async-done(((bf16[64,8,4096]{2,1,0:T(8,128)(2,1)}), bf16[64,8,4096]{2,1,0:T(8,128)(2,1)}, u32[]{:S(2)}, u32[]{:S(2)}) %all-to-all-start.3) | async-done | bytes 4194336 | tf_op jit(solution)/shard_map/all_to_all | solution.py:358
  244.8 3.5 %combine_grads.1 = bf16[128,4096]{1,0:T(8,128)(2,1)} custom-call(bf16[128,512]{1,0:T(8,128)(2,1)} %get-tuple-element.53.pick_ref, bf16[512,4096]{1,0:T(8,128)(2,1)} %bitcast.12.rows_ref), custom_call_target="tpu_custom_call" | custom-call | tf_op jit(solution)/shard_map/combine_grads/pallas_call | solution.py:448
Async XLA Ops:
  7.7 12.0 %copy-start = (bf16[1,4096,384]{2,1,0:T(8,128)(2,1)S(1)}, bf16[1,4096,384]{2,1,0:T(8,128)(2,1)}, u32[]{:S(2)}) copy-start(bf16[1,4096,384]{2,1,0:T(8,128)(2,1)} %param.11) | copy-start | bytes 9437188
  7.7 60.7 %all-to-all-start = ((bf16[64,8,4096]{2,1,0:T(8,128)(2,1)}), bf16[64,8,4096]{2,1,0:T(8,128)(2,1)}, u32[]{:S(2)}, u32[]{:S(2)}) async-start(bf16[64,8,4096]{2,1,0:T(8,128)(2,1)} %bitcast.29), calls=%async_computation | async-start | bytes 8388608 | tf_op jit(solution)/shard_map/all_to_all | solution.py:358
  19.7 9.3 %collective-permute-start = (bf16[4096,384]{1,0:T(8,128)(2,1)S(1)}, bf16[4096,384]{1,0:T(8,128)(2,1)S(1)}, u32[]{:S(2)}, u32[]{:S(2)}) collective-permute-start(bf16[4096,384]{1,0:T(8,128)(2,1)S(1)} %bitcast.20), channel_id=1, source_target_pairs={{0,64},{64,0},{1,65},{65,1},{2,66},{66,2},{3,67},{67,3},{4,68},{68... | collective-permute-start | bytes 9437192 | tf_op jit(solution)/shard_map/ppermute | solution.py:362
  19.8 10.9 %collective-permute-start.1 = (bf16[4096,384]{1,0:T(8,128)(2,1)}, bf16[4096,384]{1,0:T(8,128)(2,1)S(1)}, u32[]{:S(2)}, u32[]{:S(2)}) collective-permute-start(bf16[4096,384]{1,0:T(8,128)(2,1)} %bitcast.21), channel_id=1, source_target_pairs={{0,64},{64,0},{1,65},{65,1},{2,66},{66,2},{3,67},{67,3},{4,68},{68... | collective-permute-start | bytes 9437192 | tf_op jit(solution)/shard_map/ppermute | solution.py:362
  20.3 14.4 %collective-permute-start.2 = (bf16[384,4096]{1,0:T(8,128)(2,1)}, bf16[384,4096]{1,0:T(8,128)(2,1)S(1)}, u32[]{:S(2)}, u32[]{:S(2)}) collective-permute-start(bf16[384,4096]{1,0:T(8,128)(2,1)} %bitcast.24), channel_id=1, source_target_pairs={{0,64},{64,0},{1,65},{65,1},{2,66},{66,2},{3,67},{67,3},{4,68},{68... | collective-permute-start | bytes 9437192 | tf_op jit(solution)/shard_map/ppermute | solution.py:362
  29.0 1.7 copy-start.1
  30.7 1.7 copy-start.2
  34.7 1.7 copy-start.3
  68.4 58.4 %all-to-all-start.1 = ((bf16[64,8,4096]{2,1,0:T(8,128)(2,1)}), bf16[64,8,4096]{2,1,0:T(8,128)(2,1)}, u32[]{:S(2)}, u32[]{:S(2)}) async-start(bf16[64,8,4096]{2,1,0:T(8,128)(2,1)} %bitcast.17), calls=%async_computation.1 | async-start | bytes 8388608 | tf_op jit(solution)/shard_map/all_to_all | solution.py:358
  126.8 58.8 %all-to-all-start.2 = ((bf16[64,8,4096]{2,1,0:T(8,128)(2,1)}), bf16[64,8,4096]{2,1,0:T(8,128)(2,1)}, u32[]{:S(2)}, u32[]{:S(2)}) async-start(bf16[64,8,4096]{2,1,0:T(8,128)(2,1)} %bitcast.28), calls=%async_computation.2 | async-start | bytes 8388608 | tf_op jit(solution)/shard_map/all_to_all | solution.py:358
  136.4 63.0 %collective-permute-start.3 = (bf16[512,4096]{1,0:T(8,128)(2,1)}, bf16[512,4096]{1,0:T(8,128)(2,1)}, u32[]{:S(2)}, u32[]{:S(2)}) collective-permute-start(bf16[512,4096]{1,0:T(8,128)(2,1)} %bitcast.3.x_ref.x_near), channel_id=1, source_target_pairs={{0,64},{64,0},{1,65},{65,1},{2,66},{66,2},{3,67},{67,3},{4,68},{68... | collective-permute-start | bytes 12582920 | tf_op jit(solution)/shard_map/ppermute | solution.py:362
  136.5 75.4 %collective-permute-start.6 = (bf16[512,4096]{1,0:T(8,128)(2,1)}, bf16[512,4096]{1,0:T(8,128)(2,1)}, u32[]{:S(2)}, u32[]{:S(2)}) collective-permute-start(bf16[512,4096]{1,0:T(8,128)(2,1)} %bitcast.8.g_ref.g_near), channel_id=1, source_target_pairs={{0,64},{64,0},{1,65},{65,1},{2,66},{66,2},{3,67},{67,3},{4,68},{68... | collective-permute-start | bytes 12582920 | tf_op jit(solution)/shard_map/ppermute | solution.py:362
  185.6 6.9 %copy-start.7 = (bf16[512,384]{1,0:T(8,128)(2,1)S(1)}, bf16[512,384]{1,0:T(8,128)(2,1)}, u32[]{:S(2)}) copy-start(bf16[512,384]{1,0:T(8,128)(2,1)} %get-tuple-element.57) | copy-start | bytes 1179652
  185.6 7.0 %copy-start.6 = (bf16[512,384]{1,0:T(8,128)(2,1)S(1)}, bf16[512,384]{1,0:T(8,128)(2,1)}, u32[]{:S(2)}) copy-start(bf16[512,384]{1,0:T(8,128)(2,1)} %get-tuple-element.59) | copy-start | bytes 1179652
  185.6 7.5 %copy-start.5 = (bf16[512,384]{1,0:T(8,128)(2,1)S(1)}, bf16[512,384]{1,0:T(8,128)(2,1)}, u32[]{:S(2)}) copy-start(bf16[512,384]{1,0:T(8,128)(2,1)} %get-tuple-element.63) | copy-start | bytes 1179652
  185.6 59.2 %all-to-all-start.3 = ((bf16[64,8,4096]{2,1,0:T(8,128)(2,1)}), bf16[64,8,4096]{2,1,0:T(8,128)(2,1)}, u32[]{:S(2)}, u32[]{:S(2)}) async-start(bf16[64,8,4096]{2,1,0:T(8,128)(2,1)} %bitcast.27), calls=%async_computation.3 | async-start | bytes 8388608 | tf_op jit(solution)/shard_map/all_to_all | solution.py:358
  192.5 6.9 %collective-permute-start.4 = (bf16[512,384]{1,0:T(8,128)(2,1)S(1)}, bf16[512,384]{1,0:T(8,128)(2,1)S(1)}, u32[]{:S(2)}, u32[]{:S(2)}) collective-permute-start(bf16[512,384]{1,0:T(8,128)(2,1)S(1)} %copy-done.7), channel_id=1, source_target_pairs={{0,64},{64,0},{1,65},{65,1},{2,66},{66,2},{3,67},{67,3},{4,68},{68... | collective-permute-start | bytes 1179656 | tf_op jit(solution)/shard_map/ppermute | solution.py:362
  192.6 6.8 %collective-permute-start.5 = (bf16[512,384]{1,0:T(8,128)(2,1)S(1)}, bf16[512,384]{1,0:T(8,128)(2,1)S(1)}, u32[]{:S(2)}, u32[]{:S(2)}) collective-permute-start(bf16[512,384]{1,0:T(8,128)(2,1)S(1)} %copy-done.6), channel_id=1, source_target_pairs={{0,64},{64,0},{1,65},{65,1},{2,66},{66,2},{3,67},{67,3},{4,68},{68... | collective-permute-start | bytes 1179656 | tf_op jit(solution)/shard_map/ppermute | solution.py:362
  193.1 18.8 %collective-permute-start.7 = (bf16[512,384]{1,0:T(8,128)(2,1)S(1)}, bf16[512,384]{1,0:T(8,128)(2,1)S(1)}, u32[]{:S(2)}, u32[]{:S(2)}) collective-permute-start(bf16[512,384]{1,0:T(8,128)(2,1)S(1)} %copy-done.5), channel_id=1, source_target_pairs={{0,64},{64,0},{1,65},{65,1},{2,66},{66,2},{3,67},{67,3},{4,68},{68... | collective-permute-start | bytes 1179656 | tf_op jit(solution)/shard_map/ppermute | solution.py:362
  199.4 0.7 copy-start.8
  200.2 0.8 copy-start.9
  211.9 0.8 copy-start.4
